TPU v7x, 512 devices: a whole 4x4x16 slice. The times are simulated.
512 devices in a mesh: dp: 32 (over z, core), tensor: 16 (over x, y).
Axes of the slice: x: 4, y: 4, z: 16, core: 2. Of those that a mesh axis runs over, the one named last changes fastest.
Arguments:
- hidden_in: bfloat16 [16384, 8192], P('dp', 'tensor'), may hold values from -6 to 6
- norm_gain: float32 [8192], P('tensor'), may hold values from 0.5 to 1.5
- key_weight: bfloat16 [8192, 512], P('tensor'), as said below
- value_weight: bfloat16 [8192, 512], P('tensor'), may hold values from -0.0625 to 0.0625
- queries: bfloat16 [16384, 4096], P('dp', 'tensor'), may hold values from -8 to 8
- segments: int32 [32, 512], P('dp'), may hold values from 0 to 3, never falling along the last dimension, each value on 1 to 256 neighbouring positions
- cotangent: bfloat16 [16384, 4096], P('dp', 'tensor'), may hold values from -6 to 6
Outputs:
- attn_out: bfloat16 [16384, 4096], P('dp', 'tensor')
- grad_hidden: bfloat16 [16384, 8192], P('dp', 'tensor')
- grad_queries: bfloat16 [16384, 4096], P('dp', 'tensor')
- grad_key_weight: float32 [8192, 512], P(('tensor', 'dp'))
- grad_value_weight: float32 [8192, 512], P(('tensor', 'dp'))
- grad_gain: float32 [8192], P(('tensor', 'dp'))
Inputs may be any that keep to these rules, and one draw needn't show every extreme that they name: `segments`: segment numbers never fall along a row; each document has 1 to 256 tokens, one exactly 256. `key_weight`: entries have a standard deviation of about 8192^(-1/2) and lie within 6 such deviations.
All inputs are finite; a program needn't handle non-finite values.
Results may differ from a plain program's by a relative error of at most 0.035.
Values may be sent and summed in bfloat16 or wider, within the bound.
No kernel may reach another device: no remote copies, remote signals or barrier semaphores. Data moves between devices by JAX's collectives and lax.ppermute only.
A program may use at most 64 MiB of HBM per device.

v0:
```python
import jax
import jax.numpy as jnp
from jax import lax
from jax.sharding import PartitionSpec as P

D = 8192
HQ = 32
KVH = 4
HD = 128


ROPE_BASE = 500000.0


def angles(pos, head_size, ndim):
    half = head_size // 2
    freq = ROPE_BASE ** (-(jnp.arange(half).astype(jnp.float32) * 2.0 / head_size))
    angle = pos[:, None] * freq[None, :]
    shape = (pos.shape[0],) + (1,) * (ndim - 2) + (half,)
    return (jnp.cos(angle).reshape(shape), jnp.sin(angle).reshape(shape))


def rotate(vec, pos, sign):
    half = vec.shape[-1] // 2
    cosine, sine = angles(pos, vec.shape[-1], vec.ndim)
    first = vec[..., :half]
    second = vec[..., half:]
    return jnp.concatenate(
        [first * cosine - sign * second * sine, second * cosine + sign * first * sine], axis=-1
    )


def row_layout(seg):
    rows = seg.shape[0]
    index = jnp.arange(rows)
    same = seg[:, None] == seg[None, :]
    start = jnp.min(jnp.where(same, index[None, :], rows), axis=1)
    pos = (index - start).astype(jnp.float32)
    allowed = same & (index[None, :] <= index[:, None])
    return (pos, allowed)


def body(hidden_in, norm_gain, key_weight, value_weight, queries, segments, cotangent):
    rows = hidden_in.shape[0]
    width = key_weight.shape[1]
    group = HQ // KVH
    scale = 1.0 / HD**0.5
    tens_size = lax.axis_size("tensor")
    tens_index = lax.axis_index("tensor")
    local_heads = queries.shape[1] // HD
    kv_count = max(local_heads // group, 1)
    repeat = min(local_heads, group)
    kv_first = tens_index * local_heads // group
    sharers = max(tens_size // KVH, 1)
    in_float = hidden_in.astype(jnp.float32)
    square_sum = lax.psum(jnp.sum(in_float * in_float, axis=1), "tensor")
    inv_rms = lax.rsqrt(square_sum / D + 1e-05)
    unit = in_float * inv_rms[:, None]
    normed = (unit * norm_gain[None, :]).astype(jnp.bfloat16)
    partial_value = jnp.stack(
        [
            jnp.dot(normed, key_weight, preferred_element_type=jnp.float32),
            jnp.dot(normed, value_weight, preferred_element_type=jnp.float32),
        ],
        axis=1,
    )
    kv_both = lax.psum(partial_value.reshape(rows, 2 * width), "tensor").astype(jnp.bfloat16)
    kv_heads = kv_both.reshape(rows, 2, KVH, HD)
    key_local = lax.dynamic_slice_in_dim(kv_heads[:, 0], kv_first, kv_count, 1)
    value_local = lax.dynamic_slice_in_dim(kv_heads[:, 1], kv_first, kv_count, 1)
    pos, allowed = row_layout(segments[0])
    query_four = queries.reshape(rows, kv_count, repeat, HD)
    q_rot = rotate(query_four.astype(jnp.float32), pos, 1.0).astype(jnp.bfloat16)
    k_rot = rotate(key_local.astype(jnp.float32), pos, 1.0).astype(jnp.bfloat16)
    scores = jnp.einsum("qcrd,kcd->crqk", q_rot, k_rot, preferred_element_type=jnp.float32) * scale
    scores = jnp.where(allowed[None, None], scores, -1e30)
    top = jnp.max(scores, axis=-1, keepdims=True)
    expo = jnp.exp(scores - top)
    probs = (expo / jnp.sum(expo, axis=-1, keepdims=True)).astype(jnp.bfloat16)
    attn_out = (
        jnp.einsum("crqk,kcd->qcrd", probs, value_local, preferred_element_type=jnp.float32)
        .astype(jnp.bfloat16)
        .reshape(rows, local_heads * HD)
    )
    cot_four = cotangent.reshape(rows, kv_count, repeat, HD)
    d_probs = jnp.einsum(
        "qcrd,kcd->crqk", cot_four, value_local, preferred_element_type=jnp.float32
    )
    prob_float = probs.astype(jnp.float32)
    delta = jnp.sum(prob_float * d_probs, axis=-1, keepdims=True)
    d_scores = (prob_float * (d_probs - delta) * scale).astype(jnp.bfloat16)
    d_qrot = jnp.einsum("crqk,kcd->qcrd", d_scores, k_rot, preferred_element_type=jnp.float32)
    grad_queries = rotate(d_qrot, pos, -1.0).astype(jnp.bfloat16).reshape(rows, local_heads * HD)
    d_krot = jnp.einsum("crqk,qcrd->kcd", d_scores, q_rot, preferred_element_type=jnp.float32)
    d_key_part = rotate(d_krot, pos, -1.0)
    d_value_part = jnp.einsum("crqk,qcrd->kcd", probs, cot_four, preferred_element_type=jnp.float32)
    grad_part = jnp.stack([d_key_part, d_value_part], axis=1)
    gathered = lax.all_gather(grad_part.astype(jnp.bfloat16), "tensor", axis=2, tiled=True).astype(
        grad_part.dtype
    )
    summed = jnp.sum(gathered.reshape(rows, 2, KVH, sharers, HD), axis=3)
    kv_grad = summed.astype(jnp.bfloat16).reshape(rows, 2, width)
    d_keys = kv_grad[:, 0]
    d_values = kv_grad[:, 1]
    d_normed = jnp.dot(d_keys, key_weight.T, preferred_element_type=jnp.float32) + jnp.dot(
        d_values, value_weight.T, preferred_element_type=jnp.float32
    )
    key_term = jnp.dot(normed.T, d_keys, preferred_element_type=jnp.float32)
    value_term = jnp.dot(normed.T, d_values, preferred_element_type=jnp.float32)
    gain_term = jnp.sum(d_normed * unit, axis=0)
    grad_key, grad_value, grad_gain = (
        lax.psum_scatter(
            key_term.astype(jnp.bfloat16), "dp", scatter_dimension=0, tiled=True
        ).astype(jnp.float32),
        lax.psum_scatter(
            value_term.astype(jnp.bfloat16), "dp", scatter_dimension=0, tiled=True
        ).astype(jnp.float32),
        lax.psum_scatter(
            gain_term.astype(jnp.bfloat16), "dp", scatter_dimension=0, tiled=True
        ).astype(jnp.float32),
    )
    d_unit = d_normed * norm_gain[None, :]
    corr = lax.psum(jnp.sum(d_unit * unit, axis=1), "tensor") / D
    grad_hidden = (inv_rms[:, None] * (d_unit - unit * corr[:, None])).astype(jnp.bfloat16)
    return (attn_out, grad_hidden, grad_queries, grad_key, grad_value, grad_gain)


def solution(mesh):
    return jax.shard_map(
        body,
        mesh=mesh,
        in_specs=(
            P("dp", "tensor"),
            P("tensor"),
            P("tensor", None),
            P("tensor", None),
            P("dp", "tensor"),
            P("dp", None),
            P("dp", "tensor"),
        ),
        out_specs=(
            P("dp", "tensor"),
            P("dp", "tensor"),
            P("dp", "tensor"),
            P(("tensor", "dp"), None),
            P(("tensor", "dp"), None),
            P(("tensor", "dp")),
        ),
        check_vma=False,
    )
```

profile of v0, /device:TPU:6, one launch (start us, length us, event | category | flops | bytes accessed | tf_op | source)
XLA Modules:
  0.0 456.9 jit_solution(13171767689722365807)
XLA Ops:
  7.3 1.0 fusion.17
  8.3 1.7 compare_and_fusion
  10.0 1.2 fusion.16
  11.2 34.5 %psum.21 = f32[512]{0:T(512)S(1)} all-reduce(f32[512]{0:T(512)S(1)} %fusion.16), channel_id=1, replica_groups=mesh['dp'=32,'tensor'=16] {'tensor'}, use_global_device_ids=true, to_apply=%region_1.2 | all-reduce | flops 512 | bytes 4096 | tf_op jit(solution)/shard_map/psum | solution.py:56
  45.7 1.6 convolution_bitcast_fusion
  48.1 87.6 %all-reduce.2 = bf16[512,1024]{0,1:T(8,128)(2,1)} all-reduce(f32[512,1024]{0,1:T(8,128)S(1)} %bitcast.128), channel_id=1, replica_groups=mesh['dp'=32,'tensor'=16] {'tensor'}, use_global_device_ids=true, to_apply=%region_2.3 | all-reduce | flops 524288 | bytes 3145728 | tf_op jit(solution)/shard_map/psum | solution.py:67
  135.7 2.1 fusion.60
  138.0 1.8 broadcast_multiply_fusion
  139.8 1.2 fusion.48
  141.7 1.1 fusion.38
  143.8 1.5 fusion
  146.7 1.2 fusion.35
  148.1 0.7 pad_maximum_fusion.2
  148.9 76.0 %all-gather.2.cloned.1.call-done = bf16[512,2,16,128]{3,0,2,1:T(8,128)(2,1)} async-done(((bf16[512,2,1,128]{3,0,2,1:T(8,128)(2,1)}), bf16[512,2,16,128]{3,0,2,1:T(8,128)(2,1)}) %all-gather.2.cloned.1.call-update) | async-done | bytes 4194320 | tf_op jit(solution)/shard_map/all_gather | solution.py:98
  224.8 4.1 reduce.3
  228.9 2.3 copy.72
  231.2 2.5 convolution_convert_fusion.1
  234.0 1.5 convolution_bitcast_fusion.2
  235.5 1.2 subtract_convert_fusion
  236.9 0.9 copy.78
  237.7 1.8 copy.80
  239.5 1.2 convolution_convert_fusion.2
  240.7 0.8 copy.79
  241.6 1.3 dynamic-slice.2
  243.5 1.4 convolution_convert_fusion
  246.2 32.1 %psum.23 = f32[512]{0:T(512)S(1)} all-reduce(f32[512]{0:T(512)S(1)} %get-tuple-element.31), channel_id=1, replica_groups=mesh['dp'=32,'tensor'=16] {'tensor'}, use_global_device_ids=true, to_apply=%region_9.10 | all-reduce | flops 512 | bytes 4096 | tf_op jit(solution)/shard_map/psum | solution.py:123
  278.3 46.6 %all-reduce = bf16[512]{0:T(512)(128)(2,1)S(1)} all-reduce(bf16[512]{0:T(512)(128)(2,1)S(1)} %get-tuple-element.30), channel_id=4, replica_groups=mesh['dp'=32,'tensor'=16] {'dp'}, use_global_device_ids=true, to_apply=%region_13.14.clone | all-reduce | flops 512 | bytes 2048
  325.4 1.1 fusion.14
  326.5 14.9 %reduce-scatter.3.cloned.1.call-done = bf16[16,512]{1,0:T(8,128)(2,1)} async-done(((bf16[512,512]{1,0:T(8,128)(2,1)}), bf16[16,512]{1,0:T(8,128)(2,1)}) %reduce-scatter.3.cloned.1.call-update) | async-done | bytes 16400 | tf_op jit(solution)/shard_map/reduce_scatter | solution.py:112
  341.4 1.3 convert_element_type.149
  342.7 106.4 %reduce-scatter.5.cloned.1.call-done = bf16[16,512]{1,0:T(8,128)(2,1)} async-done(((bf16[512,512]{1,0:T(8,128)(2,1)}), bf16[16,512]{1,0:T(8,128)(2,1)}) %reduce-scatter.5.cloned.1.call-update) | async-done | bytes 16400 | tf_op jit(solution)/shard_map/reduce_scatter | solution.py:115
  449.1 1.3 convert_element_type.151
  (49 shorter events, 6.3 us)
Async XLA Ops:
  7.2 38.5 %copy-start = (bf16[512,512]{1,0:T(8,128)(2,1)S(1)}, bf16[512,512]{1,0:T(8,128)(2,1)}, u32[]{:S(2)}) copy-start(bf16[512,512]{1,0:T(8,128)(2,1)} %param.10) | copy-start | bytes 1572868
  7.2 40.1 %copy-start.1 = (bf16[512,512]{1,0:T(8,128)(2,1)S(1)}, bf16[512,512]{1,0:T(8,128)(2,1)}, u32[]{:S(2)}) copy-start(bf16[512,512]{1,0:T(8,128)(2,1)} %param.7) | copy-start | bytes 1572868
  7.2 40.1 %copy-start.9 = (f32[512]{0:T(512)S(1)}, f32[512]{0:T(512)}, u32[]{:S(2)}) copy-start(f32[512]{0:T(512)} %param.8) | copy-start | bytes 6148
  7.2 40.1 %copy-start.3 = (bf16[512,512]{1,0:T(8,128)(2,1)S(1)}, bf16[512,512]{1,0:T(8,128)(2,1)}, u32[]{:S(2)}) copy-start(bf16[512,512]{1,0:T(8,128)(2,1)} %param.9) | copy-start | bytes 1572868
  7.2 217.6 %all-gather.2.cloned.1.call-start = ((), (), s32[]{:S(2)}) async-start(), calls=%async_computation.2 | async-start | bytes 4456448 | tf_op jit(solution)/shard_map/all_gather | solution.py:98
  135.7 5.3 %copy-start.7 = (bf16[512,256]{1,0:T(8,128)(2,1)S(1)}, bf16[512,256]{1,0:T(8,128)(2,1)}, u32[]{:S(2)}) copy-start(bf16[512,256]{1,0:T(8,128)(2,1)} %param.11) | copy-start | bytes 786436
  141.0 1.7 copy-start.5
  141.3 1.5 copy-start.6
  142.8 1.0 copy-start.8
  148.8 192.5 %reduce-scatter.3.cloned.1.call-start = ((), (), s32[]{:S(2)}) async-start(), calls=%async_computation.3 | async-start | bytes 540672 | tf_op jit(solution)/shard_map/reduce_scatter | solution.py:112
  233.8 215.3 %reduce-scatter.5.cloned.1.call-start = ((), (), s32[]{:S(2)}) async-start(), calls=%async_computation.4 | async-start | bytes 540672 | tf_op jit(solution)/shard_map/reduce_scatter | solution.py:115
  236.7 6.8 %copy-start.2 = (bf16[512,2,4,128]{0,3,2,1:T(8,128)(2,1)S(1)}, bf16[512,2,4,128]{0,3,2,1:T(8,128)(2,1)}, u32[]{:S(2)}) copy-start(bf16[512,2,4,128]{0,3,2,1:T(8,128)(2,1)} %copy.72) | copy-start | bytes 3145732
  240.7 4.3 copy-start.4
Sparse Core Ops, SparseCore 0:
  148.9 75.8 all-gather.1
  233.9 107.4 reduce-scatter.2
  344.4 104.6 reduce-scatter.4
where the time goes:
time: 458 us; the launch traced here: 457 us
  blocking collectives  201 us (44%)
  waiting for transfers between devices  197 us (43%)
  other arithmetic  20.8 us (5%)
  between operations  14.7 us (3%)
  matrix products  13.3 us (3%)
  local copies, waits for them, and re-layouts  9.92 us (2%)
    reduce_scatter x1, waiting for transfers between devices, body(): lax.psum_scatter(value_term.astype(jnp.bfloat16), 'dp', scatter_dimension...  106 us
    psum x1, blocking collectives, body(): lax.psum(partial_value.reshape(rows, 2 * width), 'tensor')  87.6 us
    all_gather x1, waiting for transfers between devices, body(): lax.all_gather(grad_part.astype(jnp.bfloat16), 'tensor', axis=2, tiled=True)  76 us
    unnamed x1, blocking collectives  46.6 us
    psum x1, blocking collectives, body(): square_sum = lax.psum(jnp.sum(in_float * in_float, axis=1), 'tensor')  34.5 us
    psum x1, blocking collectives, body(): corr = lax.psum(jnp.sum(d_unit * unit, axis=1), 'tensor') / D  32.1 us
    reduce_scatter x1, waiting for transfers between devices, body(): lax.psum_scatter(key_term.astype(jnp.bfloat16), 'dp', scatter_dimension=0...  14.9 us
  transfers between devices with their start and end apart: 3, of which 3 were waited for; matrix products, arithmetic and copies ran while one was open for 3% of the time, Pallas kernels for 0%

commit v1 on v0

v1 whole, which is shorter than its diff:
```python
import functools

import jax
import jax.numpy as jnp
import numpy as np
from jax import lax
from jax.experimental import pallas as pl
from jax.experimental.pallas import tpu as pltpu
from jax.sharding import Mesh, PartitionSpec as P

D = 8192
SEQ = 512
KVH = 4
HD = 128
SCALE = 1.0 / HD**0.5
ROPE_BASE = 500000.0
Q = 128
CH = Q + 16
NT = (((1,), (1,)), ((), ()))
TN = (((0,), (0,)), ((), ()))
BF = jnp.bfloat16
F32 = jnp.float32


def rope_tables():
    half = HD // 2
    freq = np.float32(ROPE_BASE) ** (-(np.arange(half, dtype=np.float32) * np.float32(2.0 / HD)))
    angle = (np.arange(SEQ, dtype=np.float32)[:, None] * freq[None, :]).astype(np.float64)
    cos, sin = np.cos(angle), np.sin(angle)
    return (
        np.concatenate([cos, cos], axis=1).astype(np.float32),
        np.concatenate([-sin, sin], axis=1).astype(np.float32),
    )


def eye(n):
    return lax.broadcasted_iota(jnp.int32, (n, n), 0) == lax.broadcasted_iota(jnp.int32, (n, n), 1)


def to_column(row, diag):
    return jnp.sum(jnp.where(diag, row, 0.0), axis=1, keepdims=True)


def to_row(column, diag):
    return jnp.sum(jnp.where(diag, column, 0.0), axis=0, keepdims=True)


def two_halves(row):
    lead = row.astype(BF)
    rest = (row - lead.astype(F32)).astype(BF)
    return jnp.broadcast_to(jnp.concatenate([lead, rest], axis=1), (16, 2 * HD))


def from_halves(tile):
    both = tile.astype(F32)
    return both[0:1, :HD] + both[0:1, HD:]


def turn(vec, cos, sin):
    return vec * cos + pltpu.roll(vec, HD // 2, 1) * sin


def turn_back(vec, cos, sin):
    return vec * cos - pltpu.roll(vec, HD // 2, 1) * sin


def project_kernel(hid_ref, gain_ref, wk_ref, wv_ref, out_ref):
    wk = wk_ref[...]
    wv = wv_ref[...]
    ones = jnp.ones((16, hid_ref.shape[1]), BF)
    for quarter in range(SEQ // Q):
        hid = hid_ref[quarter * Q : (quarter + 1) * Q, :].astype(F32)
        scaled = (hid * gain_ref[...]).astype(BF)
        part_k = jnp.dot(scaled, wk, preferred_element_type=F32).astype(BF)
        part_v = jnp.dot(scaled, wv, preferred_element_type=F32).astype(BF)
        square = hid * hid
        lead = square.astype(BF)
        rest = (square - lead.astype(F32)).astype(BF)
        sums = lax.dot_general(ones, lead, NT, preferred_element_type=F32)
        sums += lax.dot_general(ones, rest, NT, preferred_element_type=F32)
        tile = two_halves(sums[0:1, :])
        for head in range(KVH):
            at = head * (SEQ // Q) + quarter
            cols = slice(head * HD, (head + 1) * HD)
            out_ref[at, 0:Q, 0:HD] = part_k[:, cols]
            out_ref[at, 0:Q, HD:] = part_v[:, cols]
            out_ref[at, Q:CH, :] = tile


def combine_kernel(place_ref, got_ref, cos_ref, sin_ref, out_ref):
    total = got_ref[0].astype(F32)
    for at in range(1, got_ref.shape[0]):
        total += got_ref[at].astype(F32)
    square = total[Q : Q + 1, :HD] + total[Q : Q + 1, HD:]
    inv_row = lax.rsqrt(square / D + 1e-05)
    inv = to_column(inv_row, eye(Q))
    first = pl.multiple_of(place_ref[0] * Q, Q)
    keys = (total[:Q, :HD] * inv).astype(BF).astype(F32)
    keys = turn(keys, cos_ref[pl.ds(first, Q), :], sin_ref[pl.ds(first, Q), :]).astype(BF)
    values = (total[:Q, HD:] * inv).astype(BF)
    tile = two_halves(inv_row)
    for at in range(out_ref.shape[0]):
        out_ref[at, 0:Q, 0:HD] = keys
        out_ref[at, 0:Q, HD:] = values
        out_ref[at, Q:CH, :] = tile


def attention_kernel(
    kv_ref, q_ref, cot_ref, seg_ref, cos_ref, sin_ref, out_ref, gq_ref, gkv_ref, dk_ref, dv_ref
):
    blocks = SEQ // Q
    diag = eye(Q)
    seg_rows = [seg_ref[0:1, b * Q : (b + 1) * Q].astype(F32) for b in range(blocks)]
    seg_columns = [to_column(row, diag) for row in seg_rows]
    below = lax.broadcasted_iota(jnp.int32, (Q, Q), 0) <= lax.broadcasted_iota(
        jnp.int32, (Q, Q), 1
    )
    dk_ref[...] = jnp.zeros_like(dk_ref)
    dv_ref[...] = jnp.zeros_like(dv_ref)
    for b in range(blocks):
        rows = slice(b * Q, (b + 1) * Q)
        low = max(0, b - 2)
        keys = jnp.concatenate([kv_ref[a, 0:Q, 0:HD] for a in range(low, b + 1)], axis=0)
        values = jnp.concatenate([kv_ref[a, 0:Q, HD:] for a in range(low, b + 1)], axis=0)
        cos, sin = cos_ref[rows, :], sin_ref[rows, :]
        q_rot = jnp.concatenate(
            [
                turn(q_ref[rows, h * HD : (h + 1) * HD].astype(F32), cos, sin).astype(BF)
                for h in range(2)
            ],
            axis=0,
        )
        cot = jnp.concatenate([cot_ref[rows, 0:HD], cot_ref[rows, HD:]], axis=0)
        allowed = [seg_columns[a] == seg_rows[b] for a in range(low, b)]
        allowed.append((seg_columns[b] == seg_rows[b]) & below)
        allowed = jnp.concatenate([jnp.where(a, 0.0, -1e30) for a in allowed], axis=0)
        allowed = jnp.concatenate([allowed, allowed], axis=1)
        scores = lax.dot_general(keys, q_rot, NT, preferred_element_type=F32) * SCALE
        scores = jnp.where(allowed < 0.0, -1e30, scores)
        top = jnp.max(scores, axis=0, keepdims=True)
        expo = jnp.exp(scores - top)
        probs = (expo * (1.0 / jnp.sum(expo, axis=0, keepdims=True))).astype(BF)
        d_probs = lax.dot_general(values, cot, NT, preferred_element_type=F32)
        prob_float = probs.astype(F32)
        delta = jnp.sum(prob_float * d_probs, axis=0, keepdims=True)
        d_scores = (prob_float * (d_probs - delta) * SCALE).astype(BF)
        attn = lax.dot_general(probs, values, TN, preferred_element_type=F32)
        d_q = lax.dot_general(d_scores, keys, TN, preferred_element_type=F32)
        for h in range(2):
            cols = slice(h * HD, (h + 1) * HD)
            out_ref[rows, cols] = attn[h * Q : (h + 1) * Q].astype(BF)
            gq_ref[rows, cols] = turn_back(d_q[h * Q : (h + 1) * Q], cos, sin).astype(BF)
        span = slice(low * Q, (b + 1) * Q)
        dv_ref[span, :] += jnp.dot(probs, cot, preferred_element_type=F32)
        dk_ref[span, :] += jnp.dot(d_scores, q_rot, preferred_element_type=F32)
    for b in range(blocks):
        rows = slice(b * Q, (b + 1) * Q)
        gkv_ref[b, :, 0:HD] = dk_ref[rows, :].astype(BF)
        gkv_ref[b, :, HD:] = dv_ref[rows, :].astype(BF)


def grad_sum_kernel(place_ref, got_ref, kv_ref, cos_ref, sin_ref, out_ref):
    total = got_ref[0].astype(F32)
    for at in range(1, got_ref.shape[0]):
        total += got_ref[at].astype(F32)
    own = kv_ref[0, 0:Q, :].astype(F32)
    corr = to_row(jnp.sum(total * own, axis=1, keepdims=True), eye(Q))
    first = pl.multiple_of(place_ref[0] * Q, Q)
    d_keys = turn_back(total[:, :HD], cos_ref[pl.ds(first, Q), :], sin_ref[pl.ds(first, Q), :])
    both = jnp.concatenate([d_keys, total[:, HD:]], axis=1).astype(BF)
    tile = two_halves(corr)
    for at in range(out_ref.shape[0]):
        out_ref[at, 0:Q, :] = both
        out_ref[at, Q:CH, :] = tile


def weight_kernel(place_ref, got_ref, kv_ref, hid_ref, send_ref, keep_ref, scaled_ref, raw_ref):
    blocks = SEQ // Q
    width = KVH * HD
    diag = eye(Q)
    for b in range(blocks):
        inv = to_column(from_halves(kv_ref[b, Q:CH, :]), diag)
        for head in range(KVH):
            part = (got_ref[head * blocks + b, 0:Q, :].astype(F32) * inv).astype(BF)
            cols = slice(head * HD, (head + 1) * HD)
            scaled_ref[b * Q : (b + 1) * Q, cols] = part[:, :HD]
            scaled_ref[b * Q : (b + 1) * Q, width + head * HD : width + (head + 1) * HD] = part[
                :, HD:
            ]
    scaled = scaled_ref[...]
    for f in range(hid_ref.shape[1] // HD):
        cols = slice(f * HD, (f + 1) * HD)
        raw_ref[cols, :] = lax.dot_general(
            hid_ref[:, cols], scaled, TN, preferred_element_type=F32
        ).astype(BF)
    core = place_ref[1]
    count, step = send_ref.shape[0], send_ref.shape[1]
    for at in range(count):
        mine = pl.multiple_of((2 * at + core) * step, step)
        other = pl.multiple_of((2 * at + 1 - core) * step, step)
        keep_ref[at] = raw_ref[pl.ds(mine, step), :]
        send_ref[at] = raw_ref[pl.ds(other, step), :]


def hidden_kernel(got_ref, kv_ref, hid_ref, gain_ref, wk_ref, wv_ref, out_ref):
    blocks = SEQ // Q
    diag = eye(Q)
    wk, wv = wk_ref[...], wv_ref[...]
    for b in range(blocks):
        rows = slice(b * Q, (b + 1) * Q)
        mine = [got_ref[head * blocks + b] for head in range(KVH)]
        d_keys = jnp.concatenate([m[0:Q, :HD] for m in mine], axis=1)
        d_values = jnp.concatenate([m[0:Q, HD:] for m in mine], axis=1)
        inv = to_column(from_halves(kv_ref[b, Q:CH, :]), diag)
        corr = sum(from_halves(m[Q:CH, :]) for m in mine)
        corr = to_column(corr, diag) / D
        d_normed = lax.dot_general(d_keys, wk, NT, preferred_element_type=F32)
        d_normed += lax.dot_general(d_values, wv, NT, preferred_element_type=F32)
        unit = hid_ref[rows, :].astype(F32) * inv
        out_ref[rows, :] = (inv * (d_normed * gain_ref[...] - unit * corr)).astype(BF)


def pair_kernel(keep_ref, got_ref, out_ref):
    out_ref[...] = (keep_ref[...].astype(F32) + got_ref[...].astype(F32)).astype(BF)


def finish_kernel(place_ref, got_ref, gain_ref, wk_ref, wv_ref, gk_ref, gv_ref, gg_ref):
    step = got_ref.shape[1]
    width = KVH * HD
    total = got_ref[0].astype(F32)
    for at in range(1, got_ref.shape[0]):
        total += got_ref[at].astype(F32)
    first = pl.multiple_of(place_ref[2] * step, step)
    lanes = lax.broadcasted_iota(jnp.int32, (step, gain_ref.shape[1]), 1)
    rows = lax.broadcasted_iota(jnp.int32, (step, gain_ref.shape[1]), 0)
    gain = jnp.sum(jnp.where(lanes == rows + first, gain_ref[...], 0.0), axis=1, keepdims=True)
    gk_ref[...] = total[:, :width] * gain
    gv_ref[...] = total[:, width:] * gain
    along = wk_ref[pl.ds(first, step), :].astype(F32) * total[:, :width]
    along += wv_ref[pl.ds(first, step), :].astype(F32) * total[:, width:]
    gg_ref[...] = to_row(jnp.sum(along, axis=1, keepdims=True), eye(step))


def call(kernel, out_shape, smem=0, args=0, scratch=(), name=None):
    specs = [pl.BlockSpec(memory_space=pltpu.SMEM)] * smem
    specs += [pl.BlockSpec(memory_space=pltpu.VMEM)] * args
    vmem = pl.BlockSpec(memory_space=pltpu.VMEM)
    out_specs = [vmem] * len(out_shape) if isinstance(out_shape, (list, tuple)) else vmem
    return pl.pallas_call(
        kernel,
        out_shape=out_shape,
        in_specs=specs,
        out_specs=out_specs,
        scratch_shapes=list(scratch),
        compiler_params=pltpu.CompilerParams(vmem_limit_bytes=40 * 1024 * 1024),
        name=name,
    )


def body(nz, hidden_in, norm_gain, key_weight, value_weight, queries, segments, cotangent):
    shape = jax.ShapeDtypeStruct
    width = KVH * HD
    feats = hidden_in.shape[1]
    step = feats // (2 * nz)
    cos, sin = (jnp.asarray(t) for t in rope_tables())
    gain = norm_gain.reshape(1, feats)
    core = lax.axis_index("core")
    place = jnp.stack([lax.axis_index("y"), core, lax.axis_index("z") * 2 + core]).astype(jnp.int32)

    parts = call(project_kernel, shape((16, CH, 2 * HD), BF), 0, 4, name="project")(
        hidden_in, gain, key_weight, value_weight
    )
    parts = lax.all_to_all(parts, ("x", "y"), 0, 0, tiled=True)
    own = call(combine_kernel, shape((4, CH, 2 * HD), BF), 1, 3, name="combine")(
        place, parts, cos, sin
    )
    kv = lax.all_to_all(own, "y", 0, 0, tiled=True)
    attn_out, grad_queries, grad_parts = call(
        attention_kernel,
        [shape(queries.shape, BF), shape(queries.shape, BF), shape((4, Q, 2 * HD), BF)],
        0,
        6,
        [pltpu.VMEM((SEQ, HD), F32), pltpu.VMEM((SEQ, HD), F32)],
        name="attention",
    )(kv, queries, cotangent, segments, cos, sin)
    grad_parts = lax.all_to_all(grad_parts, "y", 0, 0, tiled=True)
    grad_own = call(grad_sum_kernel, shape((16, CH, 2 * HD), BF), 1, 4, name="grad_sum")(
        place, grad_parts, own, cos, sin
    )
    grads = lax.all_to_all(grad_own, ("x", "y"), 0, 0, tiled=True)
    send, keep = call(
        weight_kernel,
        [shape((nz, step, 2 * width), BF), shape((nz, step, 2 * width), BF)],
        1,
        3,
        [pltpu.VMEM((SEQ, 2 * width), BF), pltpu.VMEM((feats, 2 * width), BF)],
        name="weight",
    )(place, grads, kv, hidden_in)
    got = lax.ppermute(send, "core", [(0, 1), (1, 0)])
    grad_hidden = call(hidden_kernel, shape(hidden_in.shape, BF), 0, 6, name="hidden")(
        grads, kv, hidden_in, gain, key_weight, value_weight
    )
    pair = call(pair_kernel, shape(keep.shape, BF), 0, 2, name="pair")(keep, got)
    rows = lax.all_to_all(pair, "z", 0, 0, tiled=True)
    grad_key, grad_value, grad_gain = call(
        finish_kernel,
        [shape((step, width), F32), shape((step, width), F32), shape((1, step), F32)],
        1,
        4,
        name="finish",
    )(place, rows, gain, key_weight, value_weight)
    return (attn_out, grad_hidden, grad_queries, grad_key, grad_value, grad_gain.reshape(step))


def solution(mesh):
    nz = mesh.devices.shape[0] // 2
    split = Mesh(mesh.devices.reshape(nz, 2, 4, 4), ("z", "core", "x", "y"))
    dp, tensor = ("z", "core"), ("x", "y")
    return jax.shard_map(
        functools.partial(body, nz),
        mesh=split,
        in_specs=(
            P(dp, tensor),
            P(tensor),
            P(tensor, None),
            P(tensor, None),
            P(dp, tensor),
            P(dp, None),
            P(dp, tensor),
        ),
        out_specs=(
            P(dp, tensor),
            P(dp, tensor),
            P(dp, tensor),
            P(tensor + dp, None),
            P(tensor + dp, None),
            P(tensor + dp),
        ),
        check_vma=False,
    )
```

time: 458 us -> 127 us (0.28)
  blocking collectives: 201 us -> 36.3 us
  waiting for transfers between devices: 197 us -> 43.5 us
  starting transfers between devices: 0.3 us -> 26.6 us
  other arithmetic: 20.8 us -> 0.08 us
  between operations: 14.7 us -> 0.73 us
  matrix products: 13.3 us -> 0 us
  Pallas kernels: 0 us -> 12.4 us
  local copies, waits for them, and re-layouts: 9.92 us -> 4.62 us
    psum x3 -> x0, blocking collectives: 154 us -> none  [the longest x1 87.6 us: body(): lax.psum(partial_value.reshape(rows, 2 * width), 'tensor')]
    reduce_scatter x2 -> x0, waiting for transfers between devices: 121 us -> none  [the longest x1 106 us: body(): lax.psum_scatter(value_term.astype(jnp.bfloat16), 'dp', scatter_dimension...]
    all_gather x1 -> x0, waiting for transfers between devices: 76 us -> none  [body(): lax.all_gather(grad_part.astype(jnp.bfloat16), 'tensor', axis=2, tiled=True)]
    unnamed x1 -> x0, blocking collectives: 46.6 us -> none
    all_to_all x0 -> x2, waiting for transfers between devices: none -> 41.6 us  [the longest x1 27 us: body(): rows = lax.all_to_all(pair, 'z', 0, 0, tiled=True)]
    all_to_all x0 -> x3, blocking collectives: none -> 36.3 us  [the longest x1 18 us: body(): grads = lax.all_to_all(grad_own, ('x', 'y'), 0, 0, tiled=True)]
    all_to_all x0 -> x2, starting transfers between devices: none -> 24.7 us  [the longest x1 15.2 us: body(): rows = lax.all_to_all(pair, 'z', 0, 0, tiled=True)]
    dot_general x12 -> x0, matrix products: 13.3 us -> none  [the longest x1 2.51 us: body(): key_term = jnp.dot(normed.T, d_keys, preferred_element_type=jnp.float32)]
  transfers between devices with their start and end apart: 3 -> 3, of which waited for: 3 -> 3; matrix products, arithmetic and copies ran while one was open for 3% -> 0% of each run, Pallas kernels for 0% -> 2%
where the time goes in v1:
time: 127 us; the launch traced here: 124 us
  waiting for transfers between devices  43.5 us (34%)
  blocking collectives  36.3 us (29%)
  starting transfers between devices  26.6 us (21%)
  Pallas kernels  12.4 us (10%)
  local copies, waits for them, and re-layouts  4.62 us (4%)
    all_to_all x1, waiting for transfers between devices, body(): rows = lax.all_to_all(pair, 'z', 0, 0, tiled=True)  27 us
    all_to_all x1, blocking collectives, body(): grads = lax.all_to_all(grad_own, ('x', 'y'), 0, 0, tiled=True)  18 us
    all_to_all x1, starting transfers between devices, body(): rows = lax.all_to_all(pair, 'z', 0, 0, tiled=True)  15.2 us
    all_to_all x1, waiting for transfers between devices, body(): parts = lax.all_to_all(parts, ('x', 'y'), 0, 0, tiled=True)  14.6 us
    all_to_all x1, starting transfers between devices, body(): parts = lax.all_to_all(parts, ('x', 'y'), 0, 0, tiled=True)  9.54 us
    all_to_all x1, blocking collectives, body(): kv = lax.all_to_all(own, 'y', 0, 0, tiled=True)  9.21 us
    all_to_all x1, blocking collectives, body(): grad_parts = lax.all_to_all(grad_parts, 'y', 0, 0, tiled=True)  9.05 us
    unnamed x28, local copies, waits for them, and re-layouts  4.62 us
  transfers between devices with their start and end apart: 3, of which 3 were waited for; matrix products, arithmetic and copies ran while one was open for 0% of the time, Pallas kernels for 2%

profile of v1, /device:TPU:6, one launch (start us, length us, event | category | flops | bytes accessed | tf_op | source)
XLA Modules:
  0.0 124.2 jit_solution(4553495591604289231)
XLA Ops:
  0.6 0.0 copy-start
  0.6 1.0 copy-done
  1.7 1.0 copy-done.2
  2.7 1.0 copy-done.4
  3.8 0.7 copy-done.11
  4.4 2.0 %project.1 = bf16[16,144,256]{2,1,0:T(8,128)(2,1)} custom-call(bf16[512,512]{1,0:T(8,128)(2,1)S(1)} %copy-done, f32[1,512]{1,0:T(1,128)S(1)} %bitcast.5, bf16[512,512]{1,0:T(8,128)(2,1)S(1)} %copy-done.2, bf16[512,512]{1,0:T(8,128)(2,1)S(1)} %copy-done.4), custom_call_target="tpu_custom_call" | custom-call | tf_op jit(solution)/shard_map/project/pallas_call | solution.py:270
  6.5 9.5 %all-to-all-start = ((bf16[16,144,256]{2,1,0:T(8,128)(2,1)}), bf16[16,144,256]{2,1,0:T(8,128)(2,1)S(1)}, u32[]{:S(2)}, u32[]{:S(2)}) async-start(bf16[16,144,256]{2,1,0:T(8,128)(2,1)} %project.1), calls=%async_computation | async-start | bytes 2359296 | tf_op jit(solution)/shard_map/all_to_all | solution.py:273
  16.0 0.1 pad_add_fusion.place_ref
  16.1 14.6 %all-to-all-done.got_ref = bf16[16,144,256]{2,1,0:T(8,128)(2,1)S(1)} async-done(((bf16[16,144,256]{2,1,0:T(8,128)(2,1)}), bf16[16,144,256]{2,1,0:T(8,128)(2,1)S(1)}, u32[]{:S(2)}, u32[]{:S(2)}) %all-to-all-start) | async-done | bytes 1179680 | tf_op jit(solution)/shard_map/all_to_all | solution.py:273
  30.8 0.0 copy-done.6
  30.8 0.0 copy-done.7
  30.8 0.8 combine.1.kv_ref
  31.5 9.2 %all_to_all.25.kv_ref = bf16[4,144,256]{2,1,0:T(8,128)(2,1)S(1)} all-to-all(bf16[4,144,256]{2,1,0:T(8,128)(2,1)S(1)} %combine.1.kv_ref), channel_id=1, replica_groups=mesh['z'=16,'core'=2,'x'=4,'y'=4] {'y'}, dimensions={0} | all-to-all | bytes 589824 | tf_op jit(solution)/shard_map/all_to_all | solution.py:277
  40.8 0.0 copy-done.9
  40.8 0.0 copy-done.10
  40.8 3.0 %attention.1 = (bf16[512,256]{1,0:T(8,128)(2,1)}, bf16[512,256]{1,0:T(8,128)(2,1)}, bf16[4,128,256]{2,1,0:T(8,128)(2,1)S(1)}) custom-call(bf16[4,144,256]{2,1,0:T(8,128)(2,1)S(1)} %all_to_all.25.kv_ref, bf16[512,256]{1,0:T(8,128)(2,1)S(1)} %copy-done.9, bf16[512,256]{1,0:T(8,128)(2,1)S(1)} %copy-done.10, s32[1,512]{1,0:T(1,128)S(1)} %copy-done.13, ...), custom_call_target="tpu_custom_call" | custom-call | tf_op jit(solution)/shard_map/attention/pallas_call | solution.py:278
  43.7 9.1 %all_to_all.26.got_ref = bf16[4,128,256]{2,1,0:T(8,128)(2,1)S(1)} all-to-all(bf16[4,128,256]{2,1,0:T(8,128)(2,1)S(1)} %get-tuple-element.15), channel_id=1, replica_groups=mesh['z'=16,'core'=2,'x'=4,'y'=4] {'y'}, dimensions={0} | all-to-all | bytes 524288 | tf_op jit(solution)/shard_map/all_to_all | solution.py:286
  52.8 0.7 grad_sum.1
  53.5 0.0 copy-start.1
  53.5 18.0 %all_to_all.27.got_ref = bf16[16,144,256]{2,1,0:T(8,128)(2,1)S(1)} all-to-all(bf16[16,144,256]{2,1,0:T(8,128)(2,1)S(1)} %grad_sum.1), channel_id=1, replica_groups=mesh['z'=16,'core'=2,'x'=4,'y'=4] {'x','y'}, dimensions={0} | all-to-all | bytes 2359296 | tf_op jit(solution)/shard_map/all_to_all | solution.py:290
  71.5 1.6 %weight.1 = (bf16[16,16,1024]{2,1,0:T(8,128)(2,1)S(1)}, bf16[16,16,1024]{2,1,0:T(8,128)(2,1)S(1)}) custom-call(s32[3]{0:T(128)S(1)} %pad_add_fusion.place_ref, bf16[16,144,256]{2,1,0:T(8,128)(2,1)S(1)} %all_to_all.27.got_ref, bf16[4,144,256]{2,1,0:T(8,128)(2,1)S(1)} %all_to_all.25.kv_ref, bf16[512,512]{1,0:T(8,128)(2,1)S(1)} %copy-done.1), custom_call_target="tpu_custom_call" | custom-call | tf_op jit(solution)/shard_map/weight/pallas_call | solution.py:291
  73.2 1.9 %collective-permute-start = (bf16[16,16,1024]{2,1,0:T(8,128)(2,1)S(1)}, bf16[16,16,1024]{2,1,0:T(8,128)(2,1)S(1)}, u32[]{:S(2)}, u32[]{:S(2)}) collective-permute-start(bf16[16,16,1024]{2,1,0:T(8,128)(2,1)S(1)} %get-tuple-element.18), channel_id=1, source_target_pairs={{0,16},{16,0},{1,17},{17,1},{2,18},{18,2},{3,19},{19,3},{4,20},{20... | collective-permute-start | bytes 1572872 | tf_op jit(solution)/shard_map/ppermute | solution.py:299
  75.1 1.9 %collective-permute-done.got_ref = bf16[16,16,1024]{2,1,0:T(8,128)(2,1)S(1)} collective-permute-done((bf16[16,16,1024]{2,1,0:T(8,128)(2,1)S(1)}, bf16[16,16,1024]{2,1,0:T(8,128)(2,1)S(1)}, u32[]{:S(2)}, u32[]{:S(2)}) %collective-permute-start) | collective-permute-done | bytes 524320 | tf_op jit(solution)/shard_map/ppermute | solution.py:299
  77.0 0.1 pair.1
  77.1 0.8 copy-done.8
  77.9 15.2 %all-to-all-start.4 = ((bf16[16,16,1024]{2,1,0:T(8,128)(2,1)}), bf16[16,16,1024]{2,1,0:T(8,128)(2,1)}, u32[]{:S(2)}, u32[]{:S(2)}) async-start(bf16[16,16,1024]{2,1,0:T(8,128)(2,1)} %copy-done.8), calls=%async_computation.4 | async-start | bytes 1048576 | tf_op jit(solution)/shard_map/all_to_all | solution.py:304
  93.1 0.0 copy-done.3
  93.1 0.0 copy-done.5
  93.1 0.0 copy-done.12
  93.1 2.3 %hidden.1 = bf16[512,512]{1,0:T(8,128)(2,1)} custom-call(bf16[16,144,256]{2,1,0:T(8,128)(2,1)S(1)} %all_to_all.27.got_ref, bf16[4,144,256]{2,1,0:T(8,128)(2,1)S(1)} %all_to_all.25.kv_ref, bf16[512,512]{1,0:T(8,128)(2,1)S(1)} %copy-done.1, f32[1,512]{1,0:T(1,128)S(1)} %bitcast.6, bf16[512,512]{1,0:T(8,128)(2,1)S(1)} %copy-done.3, bf16[512,512]{1,0:T(8,128)(2,1)S(1)} %copy-done.5), custom_call_target="tpu_custom_call" | custom-call | tf_op jit(solution)/shard_map/hidden/pallas_call | solution.py:300
  95.4 27.0 %all-to-all-done.4.got_ref = bf16[16,16,1024]{2,1,0:T(8,128)(2,1)} async-done(((bf16[16,16,1024]{2,1,0:T(8,128)(2,1)}), bf16[16,16,1024]{2,1,0:T(8,128)(2,1)}, u32[]{:S(2)}, u32[]{:S(2)}) %all-to-all-start.4) | async-done | bytes 524320 | tf_op jit(solution)/shard_map/all_to_all | solution.py:304
  122.4 1.8 %finish.1 = (f32[16,512]{1,0:T(8,128)}, f32[16,512]{1,0:T(8,128)}, f32[1,16]{1,0:T(1,128)}) custom-call(s32[3]{0:T(128)S(1)} %pad_add_fusion.place_ref, bf16[16,16,1024]{2,1,0:T(8,128)(2,1)} %all-to-all-done.4.got_ref, f32[1,512]{1,0:T(1,128)S(1)} %bitcast.7, bf16[512,512]{1,0:T(8,128)(2,1)S(1)} %copy-done.3, bf16[512,512]{1,0:T(8,128)(2,1)S(1)} %copy-done.5), custom_call_target="tpu_custom_call" | custom-call | tf_op jit(solution)/shard_map/finish/pallas_call | solution.py:305
  (14 shorter events, 0.0 us)
Async XLA Ops:
  0.6 1.0 copy-start
  1.7 1.0 copy-start.2
  2.7 1.0 copy-start.4
  3.8 0.7 copy-start.11
  6.5 24.3 %copy-start.6 = (f32[512,128]{1,0:T(8,128)S(1)}, f32[512,128]{1,0:T(8,128)}, u32[]{:S(2)}) copy-start(f32[512,128]{1,0:T(8,128)} %constant.22.clone.sin_ref) | copy-start | bytes 786436
  6.5 24.3 %copy-start.7 = (f32[512,128]{1,0:T(8,128)S(1)}, f32[512,128]{1,0:T(8,128)}, u32[]{:S(2)}) copy-start(f32[512,128]{1,0:T(8,128)} %constant.21.clone.cos_ref) | copy-start | bytes 786436
  6.5 24.3 %all-to-all-start = ((bf16[16,144,256]{2,1,0:T(8,128)(2,1)}), bf16[16,144,256]{2,1,0:T(8,128)(2,1)S(1)}, u32[]{:S(2)}, u32[]{:S(2)}) async-start(bf16[16,144,256]{2,1,0:T(8,128)(2,1)} %project.1), calls=%async_computation | async-start | bytes 2359296 | tf_op jit(solution)/shard_map/all_to_all | solution.py:273
  16.1 24.7 %copy-start.9 = (bf16[512,256]{1,0:T(8,128)(2,1)S(1)}, bf16[512,256]{1,0:T(8,128)(2,1)}, u32[]{:S(2)}) copy-start(bf16[512,256]{1,0:T(8,128)(2,1)} %q_ref.1) | copy-start | bytes 786436
  16.1 24.7 %copy-start.10 = (bf16[512,256]{1,0:T(8,128)(2,1)S(1)}, bf16[512,256]{1,0:T(8,128)(2,1)}, u32[]{:S(2)}) copy-start(bf16[512,256]{1,0:T(8,128)(2,1)} %cot_ref.1) | copy-start | bytes 786436
  16.1 24.7 %copy-start.13 = (s32[1,512]{1,0:T(1,128)S(1)}, s32[1,512]{1,0:T(1,128)}, u32[]{:S(2)}) copy-start(s32[1,512]{1,0:T(1,128)} %seg_ref.1) | copy-start | bytes 6148
  53.5 18.0 %copy-start.1 = (bf16[512,512]{1,0:T(8,128)(2,1)S(1)}, bf16[512,512]{1,0:T(8,128)(2,1)}, u32[]{:S(2)}) copy-start(bf16[512,512]{1,0:T(8,128)(2,1)} %hid_ref.5) | copy-start | bytes 1572868
  73.2 3.8 %collective-permute-start = (bf16[16,16,1024]{2,1,0:T(8,128)(2,1)S(1)}, bf16[16,16,1024]{2,1,0:T(8,128)(2,1)S(1)}, u32[]{:S(2)}, u32[]{:S(2)}) collective-permute-start(bf16[16,16,1024]{2,1,0:T(8,128)(2,1)S(1)} %get-tuple-element.18), channel_id=1, source_target_pairs={{0,16},{16,0},{1,17},{17,1},{2,18},{18,2},{3,19},{19,3},{4,20},{20... | collective-permute-start | bytes 1572872 | tf_op jit(solution)/shard_map/ppermute | solution.py:299
  77.0 16.1 %copy-start.3 = (bf16[512,512]{1,0:T(8,128)(2,1)S(1)}, bf16[512,512]{1,0:T(8,128)(2,1)}, u32[]{:S(2)}) copy-start(bf16[512,512]{1,0:T(8,128)(2,1)} %wk_ref.5) | copy-start | bytes 1572868
  77.0 16.1 %copy-start.5 = (bf16[512,512]{1,0:T(8,128)(2,1)S(1)}, bf16[512,512]{1,0:T(8,128)(2,1)}, u32[]{:S(2)}) copy-start(bf16[512,512]{1,0:T(8,128)(2,1)} %wv_ref.5) | copy-start | bytes 1572868
  77.0 16.1 %copy-start.12 = (f32[512]{0:T(512)S(1)}, f32[512]{0:T(512)}, u32[]{:S(2)}) copy-start(f32[512]{0:T(512)} %param.10) | copy-start | bytes 6148
  77.1 0.8 copy-start.8
  77.9 44.5 %all-to-all-start.4 = ((bf16[16,16,1024]{2,1,0:T(8,128)(2,1)}), bf16[16,16,1024]{2,1,0:T(8,128)(2,1)}, u32[]{:S(2)}, u32[]{:S(2)}) async-start(bf16[16,16,1024]{2,1,0:T(8,128)(2,1)} %copy-done.8), calls=%async_computation.4 | async-start | bytes 1048576 | tf_op jit(solution)/shard_map/all_to_all | solution.py:304

commit v2 on v1

v2 whole, which is shorter than its diff:
```python
import functools

import jax
import jax.numpy as jnp
import numpy as np
from jax import lax
from jax.experimental import pallas as pl
from jax.experimental.pallas import tpu as pltpu
from jax.sharding import Mesh, PartitionSpec as P

D = 8192
SEQ = 512
KVH = 4
HD = 128
SCALE = 1.0 / HD**0.5
ROPE_BASE = 500000.0
Q = 128
CH = 2 * Q + 16
NT = (((1,), (1,)), ((), ()))
TN = (((0,), (0,)), ((), ()))
BF = jnp.bfloat16
F32 = jnp.float32


def rope_tables():
    half = HD // 2
    freq = np.float32(ROPE_BASE) ** (-(np.arange(half, dtype=np.float32) * np.float32(2.0 / HD)))
    angle = (np.arange(SEQ, dtype=np.float32)[:, None] * freq[None, :]).astype(np.float64)
    cos, sin = np.cos(angle), np.sin(angle)
    return (
        np.concatenate([cos, cos], axis=1).astype(np.float32),
        np.concatenate([-sin, sin], axis=1).astype(np.float32),
    )


def eye(n):
    return lax.broadcasted_iota(jnp.int32, (n, n), 0) == lax.broadcasted_iota(jnp.int32, (n, n), 1)


def to_column(row, diag):
    return jnp.sum(jnp.where(diag, row, 0.0), axis=1, keepdims=True)


def to_row(column, diag):
    return jnp.sum(jnp.where(diag, column, 0.0), axis=0, keepdims=True)


def two_halves(row):
    lead = row.astype(BF)
    rest = (row - lead.astype(F32)).astype(BF)
    at = lax.broadcasted_iota(jnp.int32, (16, HD), 0)
    zero = jnp.zeros((), F32)
    both = jnp.where(at == 0, lead.astype(F32), jnp.where(at == 1, rest.astype(F32), zero))
    return both.astype(BF)


def from_halves(tile):
    both = tile.astype(F32)
    return both[0:1, :] + both[1:2, :]


def turn(vec, cos, sin):
    return vec * cos + pltpu.roll(vec, HD // 2, 1) * sin


def turn_back(vec, cos, sin):
    return vec * cos - pltpu.roll(vec, HD // 2, 1) * sin


def total_of(got_ref):
    total = got_ref[0].astype(F32)
    for at in range(1, got_ref.shape[0]):
        total += got_ref[at].astype(F32)
    return total


def project_kernel(
    hid_hbm, gain_hbm, wk_hbm, wv_hbm, out_hbm, hid_ref, gain_ref, wk_ref, wv_ref, out_ref, sem, out_sem
):
    quarters = SEQ // Q
    feats = hid_ref.shape[1]
    copies = [pltpu.make_async_copy(gain_hbm, gain_ref, sem.at[0])]
    for at in range(quarters):
        rows = pl.ds(at * Q, Q)
        copies.append(pltpu.make_async_copy(hid_hbm.at[rows, :], hid_ref.at[rows, :], sem.at[1 + at]))
    part = feats // 4
    for which, (src, dst) in enumerate(((wk_hbm, wk_ref), (wv_hbm, wv_ref))):
        for at in range(4):
            rows = pl.ds(at * part, part)
            copies.append(
                pltpu.make_async_copy(src.at[rows, :], dst.at[rows, :], sem.at[5 + 4 * which + at])
            )
    for copy in copies:
        copy.start()
    ones = jnp.ones((16, feats), BF)
    sent = []
    for quarter in range(quarters):
        if quarter == 0:
            copies[0].wait()
        copies[1 + quarter].wait()
        hid = hid_ref[quarter * Q : (quarter + 1) * Q, :].astype(F32)
        scaled = (hid * gain_ref[...]).astype(BF)
        square = hid * hid
        lead = square.astype(BF)
        rest = (square - lead.astype(F32)).astype(BF)
        sums = lax.dot_general(ones, lead, NT, preferred_element_type=F32)
        sums += lax.dot_general(ones, rest, NT, preferred_element_type=F32)
        tile = two_halves(sums[0:1, :])
        if quarter == 0:
            for copy in copies[5:9]:
                copy.wait()
        part_k = jnp.dot(scaled, wk_ref[...], preferred_element_type=F32).astype(BF)
        if quarter == 0:
            for copy in copies[9:13]:
                copy.wait()
        part_v = jnp.dot(scaled, wv_ref[...], preferred_element_type=F32).astype(BF)
        for head in range(KVH):
            at = head * quarters + quarter
            cols = slice(head * HD, (head + 1) * HD)
            out_ref[at, 0:Q, :] = part_k[:, cols]
            out_ref[at, Q : 2 * Q, :] = part_v[:, cols]
            out_ref[at, 2 * Q : CH, :] = tile
            copy = pltpu.make_async_copy(out_ref.at[at], out_hbm.at[at], out_sem.at[at])
            copy.start()
            sent.append(copy)
    for copy in sent:
        copy.wait()


def combine_kernel(place_ref, got_ref, cos_ref, sin_ref, out_ref):
    total = total_of(got_ref)
    square = total[2 * Q : 2 * Q + 1, :] + total[2 * Q + 1 : 2 * Q + 2, :]
    inv_row = lax.rsqrt(square / D + 1e-05)
    inv = to_column(inv_row, eye(Q))
    first = pl.multiple_of(place_ref[0] * Q, Q)
    keys = (total[:Q, :] * inv).astype(BF).astype(F32)
    keys = turn(keys, cos_ref[pl.ds(first, Q), :], sin_ref[pl.ds(first, Q), :]).astype(BF)
    values = (total[Q : 2 * Q, :] * inv).astype(BF)
    tile = two_halves(inv_row)
    for at in range(out_ref.shape[0]):
        out_ref[at, 0:Q, :] = keys
        out_ref[at, Q : 2 * Q, :] = values
        out_ref[at, 2 * Q : CH, :] = tile


def spans():
    found, first = [], 0
    for b in range(SEQ // Q):
        low = max(0, b - 2)
        found.append((low, first))
        first += (b + 1 - low) * Q
    return found, first


def attention_kernel(
    kv_ref, q_ref, cot_ref, seg_ref, cos_ref, sin_ref, gkv_ref, probs_ref, ds_ref, dk_ref, dv_ref
):
    blocks = SEQ // Q
    diag = eye(Q)
    seg_rows = [seg_ref[0:1, b * Q : (b + 1) * Q].astype(F32) for b in range(blocks)]
    seg_columns = [to_column(row, diag) for row in seg_rows]
    below = lax.broadcasted_iota(jnp.int32, (Q, Q), 0) <= lax.broadcasted_iota(
        jnp.int32, (Q, Q), 1
    )
    dk_ref[...] = jnp.zeros_like(dk_ref)
    dv_ref[...] = jnp.zeros_like(dv_ref)
    for b, (low, first) in enumerate(spans()[0]):
        rows = slice(b * Q, (b + 1) * Q)
        keys = jnp.concatenate([kv_ref[a, 0:Q, :] for a in range(low, b + 1)], axis=0)
        values = jnp.concatenate([kv_ref[a, Q : 2 * Q, :] for a in range(low, b + 1)], axis=0)
        cos, sin = cos_ref[rows, :], sin_ref[rows, :]
        q_rot = jnp.concatenate(
            [
                turn(q_ref[rows, h * HD : (h + 1) * HD].astype(F32), cos, sin).astype(BF)
                for h in range(2)
            ],
            axis=0,
        )
        cot = jnp.concatenate([cot_ref[rows, 0:HD], cot_ref[rows, HD:]], axis=0)
        allowed = [seg_columns[a] == seg_rows[b] for a in range(low, b)]
        allowed.append((seg_columns[b] == seg_rows[b]) & below)
        allowed = jnp.concatenate([jnp.where(a, 0.0, -1e30) for a in allowed], axis=0)
        allowed = jnp.concatenate([allowed, allowed], axis=1)
        scores = lax.dot_general(keys, q_rot, NT, preferred_element_type=F32) * SCALE
        scores = jnp.where(allowed < 0.0, -1e30, scores)
        top = jnp.max(scores, axis=0, keepdims=True)
        expo = jnp.exp(scores - top)
        probs = (expo * (1.0 / jnp.sum(expo, axis=0, keepdims=True))).astype(BF)
        d_probs = lax.dot_general(values, cot, NT, preferred_element_type=F32)
        prob_float = probs.astype(F32)
        delta = jnp.sum(prob_float * d_probs, axis=0, keepdims=True)
        d_scores = (prob_float * (d_probs - delta) * SCALE).astype(BF)
        span = slice(low * Q, (b + 1) * Q)
        dv_ref[span, :] += jnp.dot(probs, cot, preferred_element_type=F32)
        dk_ref[span, :] += jnp.dot(d_scores, q_rot, preferred_element_type=F32)
        kept = slice(first, first + (b + 1 - low) * Q)
        probs_ref[kept, :] = probs
        ds_ref[kept, :] = d_scores
    for b in range(blocks):
        rows = slice(b * Q, (b + 1) * Q)
        gkv_ref[b, 0:Q, :] = dk_ref[rows, :].astype(BF)
        gkv_ref[b, Q : 2 * Q, :] = dv_ref[rows, :].astype(BF)


def turned_kernel(step, place_ref, hid_ref, send_ref, keep_ref, turned_ref):
    for b in range(SEQ // Q):
        rows = slice(b * Q, (b + 1) * Q)
        turned_ref[:, rows] = hid_ref[rows, :].astype(F32).T.astype(BF)
    core = place_ref[1]
    for parity in range(2):
        for at in range(keep_ref.shape[1] // step):
            mine = pl.multiple_of((4 * at + 2 * parity + core) * step, step)
            other = pl.multiple_of((4 * at + 2 * parity + 1 - core) * step, step)
            rows = slice(at * step, (at + 1) * step)
            keep_ref[parity, rows, :] = turned_ref[pl.ds(mine, step), :]
            send_ref[parity, rows, :] = turned_ref[pl.ds(other, step), :]


def outputs_kernel(kv_ref, probs_ref, ds_ref, cos_ref, sin_ref, out_ref, gq_ref):
    for b, (low, first) in enumerate(spans()[0]):
        rows = slice(b * Q, (b + 1) * Q)
        keys = jnp.concatenate([kv_ref[a, 0:Q, :] for a in range(low, b + 1)], axis=0)
        values = jnp.concatenate([kv_ref[a, Q : 2 * Q, :] for a in range(low, b + 1)], axis=0)
        cos, sin = cos_ref[rows, :], sin_ref[rows, :]
        kept = slice(first, first + (b + 1 - low) * Q)
        attn = lax.dot_general(probs_ref[kept, :], values, TN, preferred_element_type=F32)
        d_q = lax.dot_general(ds_ref[kept, :], keys, TN, preferred_element_type=F32)
        for h in range(2):
            cols = slice(h * HD, (h + 1) * HD)
            out_ref[rows, cols] = attn[h * Q : (h + 1) * Q].astype(BF)
            gq_ref[rows, cols] = turn_back(d_q[h * Q : (h + 1) * Q], cos, sin).astype(BF)


def grad_sum_kernel(place_ref, got_ref, kv_ref, cos_ref, sin_ref, out_ref):
    total = total_of(got_ref)
    own = kv_ref[0, 0 : 2 * Q, :].astype(F32)
    both = total * own
    corr = to_row(jnp.sum(both[:Q] + both[Q:], axis=1, keepdims=True), eye(Q))
    first = pl.multiple_of(place_ref[0] * Q, Q)
    d_keys = turn_back(total[:Q, :], cos_ref[pl.ds(first, Q), :], sin_ref[pl.ds(first, Q), :])
    d_keys = d_keys.astype(BF)
    d_values = total[Q:, :].astype(BF)
    tile = two_halves(corr)
    for at in range(out_ref.shape[0]):
        out_ref[at, 0:Q, :] = d_keys
        out_ref[at, Q : 2 * Q, :] = d_values
        out_ref[at, 2 * Q : CH, :] = tile


def weight_kernel(got_ref, kv_ref, turned_ref, out_ref, grads_ref):
    blocks = SEQ // Q
    width = KVH * HD
    for b in range(blocks):
        rows = slice(b * Q, (b + 1) * Q)
        for head in range(KVH):
            at = head * blocks + b
            grads_ref[rows, head * HD : (head + 1) * HD] = got_ref[at, 0:Q, :]
            grads_ref[rows, width + head * HD : width + (head + 1) * HD] = got_ref[at, Q : 2 * Q, :]
    inv = [from_halves(kv_ref[b, 2 * Q : CH, :]) for b in range(blocks)]
    inv = jnp.concatenate(inv, axis=1)
    for parity in range(2):
        unit = (turned_ref[parity].astype(F32) * inv).astype(BF)
        product = jnp.dot(unit, grads_ref[...], preferred_element_type=F32)
        out_ref[parity] = product.astype(BF)


def hidden_kernel(got_ref, kv_ref, hid_ref, gain_ref, wk_ref, wv_ref, out_ref):
    blocks = SEQ // Q
    diag = eye(Q)
    wk, wv = wk_ref[...], wv_ref[...]
    for b in range(blocks):
        rows = slice(b * Q, (b + 1) * Q)
        mine = [got_ref[head * blocks + b] for head in range(KVH)]
        d_keys = jnp.concatenate([m[0:Q] for m in mine], axis=1)
        d_values = jnp.concatenate([m[Q : 2 * Q] for m in mine], axis=1)
        inv = to_column(from_halves(kv_ref[b, 2 * Q : CH, :]), diag)
        corr = sum(from_halves(m[2 * Q : CH]) for m in mine)
        corr = to_column(corr, diag) / D
        d_normed = lax.dot_general(d_keys, wk, NT, preferred_element_type=F32)
        d_normed += lax.dot_general(d_values, wv, NT, preferred_element_type=F32)
        unit = hid_ref[rows, :].astype(F32) * inv
        out_ref[rows, :] = (inv * (d_normed * gain_ref[...] - unit * corr)).astype(BF)


def pair_kernel(place_ref, keep_ref, got_ref, out_ref):
    at = 1 - place_ref[3]
    out_ref[...] = (keep_ref[at].astype(F32) + got_ref[at].astype(F32)).astype(BF)


def four_kernel(place_ref, keep_ref, got_ref, next_ref, out_ref):
    at = place_ref[3]
    total = keep_ref[at].astype(F32) + got_ref[at].astype(F32) + next_ref[...].astype(F32)
    out_ref[...] = total.astype(BF)


def own_rows_kernel(place_ref, gain_ref, wk_ref, wv_ref, out_ref):
    step, width = out_ref.shape[0], KVH * HD
    first = pl.multiple_of(place_ref[2] * step, step)
    lanes = lax.broadcasted_iota(jnp.int32, (step, gain_ref.shape[1]), 1)
    rows = lax.broadcasted_iota(jnp.int32, (step, gain_ref.shape[1]), 0)
    gain = jnp.sum(jnp.where(lanes == rows + first, gain_ref[...], 0.0), axis=1, keepdims=True)
    out_ref[:, 0:width] = wk_ref[pl.ds(first, step), :].astype(F32)
    out_ref[:, width : 2 * width] = wv_ref[pl.ds(first, step), :].astype(F32)
    out_ref[:, 2 * width :] = jnp.broadcast_to(gain, (step, HD))


def finish_kernel(got_ref, rows_ref, gk_ref, gv_ref, gg_ref):
    step, width = gk_ref.shape
    total = total_of(got_ref)
    gain = rows_ref[:, 2 * width : 2 * width + 1]
    gk_ref[...] = total[:, :width] * gain
    gv_ref[...] = total[:, width:] * gain
    along = rows_ref[:, 0 : 2 * width] * total
    gg_ref[...] = to_row(jnp.sum(along, axis=1, keepdims=True), eye(step))


VMEM = pl.BlockSpec(memory_space=pltpu.VMEM)
SMEM = pl.BlockSpec(memory_space=pltpu.SMEM)
HBM = pl.BlockSpec(memory_space=pltpu.HBM)


def call(kernel, name, out_shape, in_specs, out_specs=None, scratch=(), cost=None, grant=16):
    many = isinstance(out_shape, (list, tuple))
    if out_specs is None:
        out_specs = [VMEM] * len(out_shape) if many else VMEM
    flops, size = cost
    return pl.pallas_call(
        kernel,
        out_shape=out_shape,
        in_specs=in_specs,
        out_specs=out_specs,
        scratch_shapes=list(scratch),
        compiler_params=pltpu.CompilerParams(vmem_limit_bytes=grant * 1024 * 1024),
        cost_estimate=pl.CostEstimate(flops=int(flops), bytes_accessed=int(size), transcendentals=0),
        name=name,
    )


def body(nz, hidden_in, norm_gain, key_weight, value_weight, queries, segments, cotangent):
    shape = jax.ShapeDtypeStruct
    width = KVH * HD
    feats = hidden_in.shape[1]
    step = feats // (2 * nz)
    quarter = feats // 4
    blocks = SEQ // Q
    kept = spans()[1]
    dma = pltpu.SemaphoreType.DMA
    cos, sin = (jnp.asarray(t) for t in rope_tables())
    gain = norm_gain.reshape(1, feats)
    core, parity = lax.axis_index("core"), lax.axis_index("zl")
    at = (lax.axis_index("zh") * 2 + parity) * 2 + core
    place = jnp.stack([lax.axis_index("y"), core, at, parity]).astype(jnp.int32)

    parts = call(
        project_kernel,
        "project",
        shape((KVH * blocks, CH, HD), BF),
        [HBM] * 4,
        HBM,
        [
            pltpu.VMEM((SEQ, feats), BF),
            pltpu.VMEM((1, feats), F32),
            pltpu.VMEM((feats, width), BF),
            pltpu.VMEM((feats, width), BF),
            pltpu.VMEM((KVH * blocks, CH, HD), BF),
            dma((13,)),
            dma((KVH * blocks,)),
        ],
        cost=(4 * SEQ * feats * width, 2.5e6),
        grant=60,
    )(hidden_in, gain, key_weight, value_weight)
    parts, hidden, place = lax.optimization_barrier((parts, hidden_in, place))
    turned_send, turned_keep = call(
        functools.partial(turned_kernel, step),
        "turned",
        [shape((2, quarter, SEQ), BF)] * 2,
        [SMEM, VMEM],
        scratch=[pltpu.VMEM((feats, SEQ), BF)],
        cost=(SEQ * feats, 1.5e6),
    )(place, hidden)
    own_rows = call(
        own_rows_kernel,
        "own_rows",
        shape((step, 2 * width + HD), F32),
        [SMEM] + [VMEM] * 3,
        cost=(SEQ * feats, 1e6),
    )(place, gain, key_weight, value_weight)
    parts = lax.all_to_all(parts, ("x", "y"), 0, 0, tiled=True)
    parts, turned_send, turned_keep, own_rows = lax.optimization_barrier(
        (parts, turned_send, turned_keep, own_rows)
    )
    own = call(
        combine_kernel,
        "combine",
        shape((blocks, CH, HD), BF),
        [SMEM] + [VMEM] * 3,
        cost=(16 * CH * HD, 1.5e6),
    )(place, parts, cos, sin)
    kv = lax.all_to_all(own, "y", 0, 0, tiled=True)
    grad_parts, probs, d_scores = call(
        attention_kernel,
        "attention",
        [shape((blocks, 2 * Q, HD), BF), shape((kept, 2 * Q), BF), shape((kept, 2 * Q), BF)],
        [VMEM] * 6,
        scratch=[pltpu.VMEM((SEQ, HD), F32), pltpu.VMEM((SEQ, HD), F32)],
        cost=(8 * kept * 2 * Q * HD, 2e6),
    )(kv, queries, cotangent, segments, cos, sin)
    grad_parts = lax.all_to_all(grad_parts, "y", 0, 0, tiled=True)
    grad_own = call(
        grad_sum_kernel,
        "grad_sum",
        shape((KVH * blocks, CH, HD), BF),
        [SMEM] + [VMEM] * 4,
        cost=(16 * CH * HD, 1.5e6),
    )(place, grad_parts, own, cos, sin)
    grads = lax.all_to_all(grad_own, ("x", "y"), 0, 0, tiled=True)

    def product(turned, name):
        return call(
            weight_kernel,
            name,
            shape((2, quarter, 2 * width), BF),
            [VMEM] * 3,
            scratch=[pltpu.VMEM((SEQ, 2 * width), BF)],
            cost=(4 * SEQ * feats // 2 * width, 2e6),
        )(grads, kv, turned)

    swap = [(0, 1), (1, 0)]
    send = product(turned_send, "weight_send")
    send, turned_keep = lax.optimization_barrier((send, turned_keep))
    got = lax.ppermute(send, "core", swap)
    keep = product(turned_keep, "weight_keep")
    pair = call(
        pair_kernel,
        "pair",
        shape((quarter, 2 * width), BF),
        [SMEM] + [VMEM] * 2,
        cost=(quarter * 2 * width, 1e6),
    )(place, keep, got)
    pair, probs, grads = lax.optimization_barrier((pair, probs, grads))
    got_pair = lax.ppermute(pair, "zl", swap)
    grad_hidden = call(
        hidden_kernel,
        "hidden",
        shape(hidden_in.shape, BF),
        [VMEM] * 6,
        cost=(4 * SEQ * feats * width, 4e6),
    )(grads, kv, hidden_in, gain, key_weight, value_weight)
    attn_out, grad_queries = call(
        outputs_kernel,
        "outputs",
        [shape(queries.shape, BF), shape(queries.shape, BF)],
        [VMEM] * 5,
        cost=(4 * kept * 2 * Q * HD, 2e6),
    )(kv, probs, d_scores, cos, sin)
    got_pair, grad_hidden, attn_out, grad_queries = lax.optimization_barrier(
        (got_pair, grad_hidden, attn_out, grad_queries)
    )
    four = call(
        four_kernel,
        "four",
        shape((quarter, 2 * width), BF),
        [SMEM] + [VMEM] * 3,
        cost=(quarter * 2 * width, 1e6),
    )(place, keep, got, got_pair)
    rows = lax.all_to_all(four.reshape(nz // 2, step, 2 * width), "zh", 0, 0, tiled=True)
    grad_key, grad_value, grad_gain = call(
        finish_kernel,
        "finish",
        [shape((step, width), F32), shape((step, width), F32), shape((1, step), F32)],
        [VMEM] * 2,
        cost=(quarter * 2 * width, 1e6),
    )(rows, own_rows)
    return (attn_out, grad_hidden, grad_queries, grad_key, grad_value, grad_gain.reshape(step))


def solution(mesh):
    nz = mesh.devices.shape[0] // 2
    split = Mesh(mesh.devices.reshape(nz // 2, 2, 2, 4, 4), ("zh", "zl", "core", "x", "y"))
    dp, tensor = ("zh", "zl", "core"), ("x", "y")
    return jax.shard_map(
        functools.partial(body, nz),
        mesh=split,
        in_specs=(
            P(dp, tensor),
            P(tensor),
            P(tensor, None),
            P(tensor, None),
            P(dp, tensor),
            P(dp, None),
            P(dp, tensor),
        ),
        out_specs=(
            P(dp, tensor),
            P(dp, tensor),
            P(dp, tensor),
            P(tensor + dp, None),
            P(tensor + dp, None),
            P(tensor + dp),
        ),
        check_vma=False,
    )
```

time: 127 us -> 121 us (0.953); the launches traced: 124 us -> 120 us
  blocking collectives: 36.3 us -> 71.1 us
  waiting for transfers between devices: 43.5 us -> 15.7 us
  starting transfers between devices: 26.6 us -> 15.2 us
  local copies, waits for them, and re-layouts: 4.62 us -> 1.13 us
  Pallas kernels: 12.4 us -> 15.5 us
    all_to_all x0 -> x1, blocking collectives: none -> 35.5 us  [body(): lax.all_to_all(four.reshape(nz // 2, step, 2 * width), 'zh', 0, 0, tiled=...]
    all_to_all x1 -> x0, waiting for transfers between devices: 27 us -> none  [body(): rows = lax.all_to_all(pair, 'z', 0, 0, tiled=True)]
    all_to_all x1 -> x0, starting transfers between devices: 15.2 us -> none  [body(): rows = lax.all_to_all(pair, 'z', 0, 0, tiled=True)]
    ppermute x1 -> x2, starting transfers between devices: 1.92 us -> 5.65 us  [the longest x1 3.73 us: body(): got_pair = lax.ppermute(pair, 'zl', swap)]
    unnamed x28 -> x22, local copies, waits for them, and re-layouts: 4.62 us -> 1.13 us
    all_to_all x1, waiting for transfers between devices: 14.6 us -> 11.4 us  [body(): parts = lax.all_to_all(parts, ('x', 'y'), 0, 0, tiled=True)]
    pallas_call x8 -> x13, Pallas kernels: 12.4 us -> 15.5 us  [the longest x1 3.94 us: body(): call(project_kernel, 'project', shape((KVH * blocks, CH, HD), BF), [HBM]...]
    ppermute x1 -> x2, waiting for transfers between devices: 1.88 us -> 4.24 us  [the longest x1 2.97 us: body(): got_pair = lax.ppermute(pair, 'zl', swap)]
  transfers between devices with their start and end apart: 3 -> 3, of which waited for: 3 -> 3; matrix products, arithmetic and copies ran while one was open for 0% -> 0% of each run, Pallas kernels for 2% -> 5%
where the time goes in v2:
time: 121 us; the launch traced here: 120 us
  blocking collectives  71.1 us (59%)
  waiting for transfers between devices  15.7 us (13%)
  Pallas kernels  15.5 us (13%)
  starting transfers between devices  15.2 us (13%)
    all_to_all x1, blocking collectives, body(): lax.all_to_all(four.reshape(nz // 2, step, 2 * width), 'zh', 0, 0, tiled=...  35.5 us
    all_to_all x1, blocking collectives, body(): grads = lax.all_to_all(grad_own, ('x', 'y'), 0, 0, tiled=True)  17.4 us
    all_to_all x1, waiting for transfers between devices, body(): parts = lax.all_to_all(parts, ('x', 'y'), 0, 0, tiled=True)  11.4 us
    all_to_all x1, starting transfers between devices, body(): parts = lax.all_to_all(parts, ('x', 'y'), 0, 0, tiled=True)  9.55 us
    all_to_all x1, blocking collectives, body(): kv = lax.all_to_all(own, 'y', 0, 0, tiled=True)  9.11 us
    all_to_all x1, blocking collectives, body(): grad_parts = lax.all_to_all(grad_parts, 'y', 0, 0, tiled=True)  9.07 us
    pallas_call x1, Pallas kernels, body(): call(project_kernel, 'project', shape((KVH * blocks, CH, HD), BF), [HBM]...  3.94 us
    ppermute x1, starting transfers between devices, body(): got_pair = lax.ppermute(pair, 'zl', swap)  3.73 us
  transfers between devices with their start and end apart: 3, of which 3 were waited for; matrix products, arithmetic and copies ran while one was open for 0% of the time, Pallas kernels for 5%

profile of v2, /device:TPU:6, one launch (start us, length us, event | category | flops | bytes accessed | tf_op | source)
XLA Modules:
  0.0 119.5 jit_solution(5645279401873179323)
XLA Ops:
  0.6 0.1 pad_add_fusion.place_ref
  0.7 3.9 %project.1 = bf16[16,272,128]{2,1,0:T(8,128)(2,1)} custom-call(bf16[512,512]{1,0:T(8,128)(2,1)} %hid_ref.2, f32[1,512]{1,0:T(1,128)} %bitcast.8, bf16[512,512]{1,0:T(8,128)(2,1)} %wk_ref.3, bf16[512,512]{1,0:T(8,128)(2,1)} %wv_ref.3), custom_call_target="tpu_custom_call" | custom-call | flops 536870912 | bytes 2500000 | tf_op jit(solution)/shard_map/project/pallas_call | solution.py:354
  4.7 0.0 copy-start.1
  4.7 0.0 copy-start.9
  4.7 9.6 %all-to-all-start = ((bf16[16,272,128]{2,1,0:T(8,128)(2,1)}), bf16[16,272,128]{2,1,0:T(8,128)(2,1)S(1)}, u32[]{:S(2)}, u32[]{:S(2)}) async-start(bf16[16,272,128]{2,1,0:T(8,128)(2,1)} %project.1), calls=%async_computation | async-start | bytes 2228224 | tf_op jit(solution)/shard_map/all_to_all | solution.py:388
  14.3 0.0 copy-start.3
  14.3 0.0 copy-start.4
  14.3 0.6 own_rows.1.rows_ref
  15.0 0.4 copy-done
  15.3 0.8 turned.1
  16.1 0.7 copy-done.5
  16.8 11.4 %all-to-all-done.got_ref = bf16[16,272,128]{2,1,0:T(8,128)(2,1)S(1)} async-done(((bf16[16,272,128]{2,1,0:T(8,128)(2,1)}), bf16[16,272,128]{2,1,0:T(8,128)(2,1)S(1)}, u32[]{:S(2)}, u32[]{:S(2)}) %all-to-all-start) | async-done | bytes 1114144 | tf_op jit(solution)/shard_map/all_to_all | solution.py:388
  28.3 0.0 copy-start.10
  28.3 0.8 combine.1.kv_ref
  29.1 9.1 %all_to_all.25.kv_ref = bf16[4,272,128]{2,1,0:T(8,128)(2,1)S(1)} all-to-all(bf16[4,272,128]{2,1,0:T(8,128)(2,1)S(1)} %combine.1.kv_ref), channel_id=1, replica_groups=mesh['zh'=8,'zl'=2,'core'=2,'x'=4,'y'=4] {'y'}, dimensions={0} | all-to-all | bytes 557056 | tf_op jit(solution)/shard_map/all_to_all | solution.py:399
  38.2 1.9 %attention.1 = (bf16[4,256,128]{2,1,0:T(8,128)(2,1)S(1)}, bf16[1152,256]{1,0:T(8,128)(2,1)S(1)}, bf16[1152,256]{1,0:T(8,128)(2,1)S(1)}) custom-call(bf16[4,272,128]{2,1,0:T(8,128)(2,1)S(1)} %all_to_all.25.kv_ref, bf16[512,256]{1,0:T(8,128)(2,1)S(1)} %copy-done.7, bf16[512,256]{1,0:T(8,128)(2,1)S(1)} %copy-done.8, s32[1,512]{1,0:T(1,128)S(1)} %copy-done.10, ...), custom_call_target="tpu_custom_call" | custom-call | flops 301989888 | bytes 2000000 | tf_op jit(solution)/shard_map/attention/pallas_call | solution.py:400
  40.1 9.1 %all_to_all.26.got_ref = bf16[4,256,128]{2,1,0:T(8,128)(2,1)S(1)} all-to-all(bf16[4,256,128]{2,1,0:T(8,128)(2,1)S(1)} %get-tuple-element.38), channel_id=1, replica_groups=mesh['zh'=8,'zl'=2,'core'=2,'x'=4,'y'=4] {'y'}, dimensions={0} | all-to-all | bytes 524288 | tf_op jit(solution)/shard_map/all_to_all | solution.py:408
  49.1 0.7 grad_sum.1
  49.8 0.0 copy-start.6
  49.8 17.4 %all_to_all.27.got_ref = bf16[16,272,128]{2,1,0:T(8,128)(2,1)S(1)} all-to-all(bf16[16,272,128]{2,1,0:T(8,128)(2,1)S(1)} %grad_sum.1), channel_id=1, replica_groups=mesh['zh'=8,'zl'=2,'core'=2,'x'=4,'y'=4] {'x','y'}, dimensions={0} | all-to-all | bytes 2228224 | tf_op jit(solution)/shard_map/all_to_all | solution.py:416
  67.3 0.6 weight_send.1
  67.9 1.9 %collective-permute-start = (bf16[2,128,1024]{2,1,0:T(8,128)(2,1)S(1)}, bf16[2,128,1024]{2,1,0:T(8,128)(2,1)S(1)}, u32[]{:S(2)}, u32[]{:S(2)}) collective-permute-start(bf16[2,128,1024]{2,1,0:T(8,128)(2,1)S(1)} %weight_send.1), channel_id=1, source_target_pairs={{0,16},{16,0},{1,17},{17,1},{2,18},{18,2},{3,19},{19,3},{4,20},{20... | collective-permute-start | bytes 1572872 | tf_op jit(solution)/shard_map/ppermute | solution.py:431
  69.8 0.6 weight_keep.1.keep_ref
  70.4 1.3 %collective-permute-done.got_ref = bf16[2,128,1024]{2,1,0:T(8,128)(2,1)S(1)} collective-permute-done((bf16[2,128,1024]{2,1,0:T(8,128)(2,1)S(1)}, bf16[2,128,1024]{2,1,0:T(8,128)(2,1)S(1)}, u32[]{:S(2)}, u32[]{:S(2)}) %collective-permute-start) | collective-permute-done | bytes 524320 | tf_op jit(solution)/shard_map/ppermute | solution.py:431
  71.7 0.6 pair.1
  72.3 3.7 %collective-permute-start.1 = (bf16[128,1024]{1,0:T(8,128)(2,1)S(1)}, bf16[128,1024]{1,0:T(8,128)(2,1)S(1)}, u32[]{:S(2)}, u32[]{:S(2)}) collective-permute-start(bf16[128,1024]{1,0:T(8,128)(2,1)S(1)} %pair.1), channel_id=1, source_target_pairs={{0,32},{32,0},{1,33},{33,1},{2,34},{34,2},{3,35},{35,3},{4,36},{36... | collective-permute-start | bytes 786440 | tf_op jit(solution)/shard_map/ppermute | solution.py:441
  76.0 1.3 %outputs.1 = (bf16[512,256]{1,0:T(8,128)(2,1)}, bf16[512,256]{1,0:T(8,128)(2,1)}) custom-call(bf16[4,272,128]{2,1,0:T(8,128)(2,1)S(1)} %all_to_all.25.kv_ref, bf16[1152,256]{1,0:T(8,128)(2,1)S(1)} %get-tuple-element.46.probs_ref, bf16[1152,256]{1,0:T(8,128)(2,1)S(1)} %get-tuple-element.47.ds_ref, f32[512,128]{1,0:T(8,128)S(1)} %copy-done.4, ...), custom_call_target="tpu_custom_call" | custom-call | flops 150994944 | bytes 2000000 | tf_op jit(solution)/shard_map/outputs/pallas_call | solution.py:449
  77.3 2.3 %hidden.1 = bf16[512,512]{1,0:T(8,128)(2,1)} custom-call(bf16[16,272,128]{2,1,0:T(8,128)(2,1)S(1)} %all_to_all.27.got_ref, bf16[4,272,128]{2,1,0:T(8,128)(2,1)S(1)} %all_to_all.25.kv_ref, bf16[512,512]{1,0:T(8,128)(2,1)S(1)} %copy-done, f32[1,512]{1,0:T(1,128)S(1)} %bitcast.10, bf16[512,512]{1,0:T(8,128)(2,1)S(1)} %copy-done.1, bf16[512,512]{1,0:T(8,128)(2,1)S(1)} %copy-done.2), custom_call_target="tpu_custom_call" | custom-call | flops 536870912 | bytes 4000000 | tf_op jit(solution)/shard_map/hidden/pallas_call | solution.py:442
  79.6 3.0 %collective-permute-done.1.next_ref = bf16[128,1024]{1,0:T(8,128)(2,1)S(1)} collective-permute-done((bf16[128,1024]{1,0:T(8,128)(2,1)S(1)}, bf16[128,1024]{1,0:T(8,128)(2,1)S(1)}, u32[]{:S(2)}, u32[]{:S(2)}) %collective-permute-start.1) | collective-permute-done | bytes 262176 | tf_op jit(solution)/shard_map/ppermute | solution.py:441
  82.6 0.6 four.1
  83.3 35.5 %all_to_all.28.got_ref = bf16[8,16,1024]{2,1,0:T(8,128)(2,1)S(1)} all-to-all(bf16[8,16,1024]{2,1,0:T(8,128)(2,1)S(1)} %bitcast.7), channel_id=1, replica_groups=mesh['zh'=8,'zl'=2,'core'=2,'x'=4,'y'=4] {'zh'}, dimensions={0} | all-to-all | bytes 524288 | tf_op jit(solution)/shard_map/all_to_all | solution.py:466
  118.8 0.7 finish.1
  (14 shorter events, 0.0 us)
Async XLA Ops:
  4.7 9.6 %copy-start.1 = (bf16[512,512]{1,0:T(8,128)(2,1)S(1)}, bf16[512,512]{1,0:T(8,128)(2,1)}, u32[]{:S(2)}) copy-start(bf16[512,512]{1,0:T(8,128)(2,1)} %wk_ref.3) | copy-start | bytes 1572868
  4.7 9.6 %copy-start.2 = (bf16[512,512]{1,0:T(8,128)(2,1)S(1)}, bf16[512,512]{1,0:T(8,128)(2,1)}, u32[]{:S(2)}) copy-start(bf16[512,512]{1,0:T(8,128)(2,1)} %wv_ref.3) | copy-start | bytes 1572868
  4.7 9.6 %copy-start.9 = (f32[512]{0:T(512)S(1)}, f32[512]{0:T(512)}, u32[]{:S(2)}) copy-start(f32[512]{0:T(512)} %param.10) | copy-start | bytes 6148
  4.7 23.5 %all-to-all-start = ((bf16[16,272,128]{2,1,0:T(8,128)(2,1)}), bf16[16,272,128]{2,1,0:T(8,128)(2,1)S(1)}, u32[]{:S(2)}, u32[]{:S(2)}) async-start(bf16[16,272,128]{2,1,0:T(8,128)(2,1)} %project.1), calls=%async_computation | async-start | bytes 2228224 | tf_op jit(solution)/shard_map/all_to_all | solution.py:388
  14.3 1.0 copy-start
  14.3 14.0 %copy-start.3 = (f32[512,128]{1,0:T(8,128)S(1)}, f32[512,128]{1,0:T(8,128)}, u32[]{:S(2)}) copy-start(f32[512,128]{1,0:T(8,128)} %constant.27.clone.sin_ref) | copy-start | bytes 786436
  14.3 13.9 %copy-start.4 = (f32[512,128]{1,0:T(8,128)S(1)}, f32[512,128]{1,0:T(8,128)}, u32[]{:S(2)}) copy-start(f32[512,128]{1,0:T(8,128)} %constant.26.clone.cos_ref) | copy-start | bytes 786436
  16.1 0.7 copy-start.5
  28.2 9.9 %copy-start.7 = (bf16[512,256]{1,0:T(8,128)(2,1)S(1)}, bf16[512,256]{1,0:T(8,128)(2,1)}, u32[]{:S(2)}) copy-start(bf16[512,256]{1,0:T(8,128)(2,1)} %q_ref.1) | copy-start | bytes 786436
  28.3 9.9 %copy-start.8 = (bf16[512,256]{1,0:T(8,128)(2,1)S(1)}, bf16[512,256]{1,0:T(8,128)(2,1)}, u32[]{:S(2)}) copy-start(bf16[512,256]{1,0:T(8,128)(2,1)} %cot_ref.1) | copy-start | bytes 786436
  28.3 9.9 %copy-start.10 = (s32[1,512]{1,0:T(1,128)S(1)}, s32[1,512]{1,0:T(1,128)}, u32[]{:S(2)}) copy-start(s32[1,512]{1,0:T(1,128)} %seg_ref.1) | copy-start | bytes 6148
  49.8 17.4 %copy-start.6 = (bf16[2,128,512]{2,1,0:T(8,128)(2,1)S(1)}, bf16[2,128,512]{2,1,0:T(8,128)(2,1)}, u32[]{:S(2)}) copy-start(bf16[2,128,512]{2,1,0:T(8,128)(2,1)} %copy-done.5) | copy-start | bytes 786436
  67.9 3.8 %collective-permute-start = (bf16[2,128,1024]{2,1,0:T(8,128)(2,1)S(1)}, bf16[2,128,1024]{2,1,0:T(8,128)(2,1)S(1)}, u32[]{:S(2)}, u32[]{:S(2)}) collective-permute-start(bf16[2,128,1024]{2,1,0:T(8,128)(2,1)S(1)} %weight_send.1), channel_id=1, source_target_pairs={{0,16},{16,0},{1,17},{17,1},{2,18},{18,2},{3,19},{19,3},{4,20},{20... | collective-permute-start | bytes 1572872 | tf_op jit(solution)/shard_map/ppermute | solution.py:431
  72.3 10.3 %collective-permute-start.1 = (bf16[128,1024]{1,0:T(8,128)(2,1)S(1)}, bf16[128,1024]{1,0:T(8,128)(2,1)S(1)}, u32[]{:S(2)}, u32[]{:S(2)}) collective-permute-start(bf16[128,1024]{1,0:T(8,128)(2,1)S(1)} %pair.1), channel_id=1, source_target_pairs={{0,32},{32,0},{1,33},{33,1},{2,34},{34,2},{3,35},{35,3},{4,36},{36... | collective-permute-start | bytes 786440 | tf_op jit(solution)/shard_map/ppermute | solution.py:441

commit v3 on v2

v3 whole, which is shorter than its diff:
```python
import functools

import jax
import jax.numpy as jnp
import numpy as np
from jax import lax
from jax.experimental import pallas as pl
from jax.experimental.pallas import tpu as pltpu
from jax.sharding import Mesh, PartitionSpec as P

D = 8192
SEQ = 512
KVH = 4
HD = 128
SCALE = 1.0 / HD**0.5
ROPE_BASE = 500000.0
Q = 128
CH = 2 * Q + 16
NT = (((1,), (1,)), ((), ()))
TN = (((0,), (0,)), ((), ()))
BF = jnp.bfloat16
F32 = jnp.float32


def rope_tables():
    half = HD // 2
    freq = np.float32(ROPE_BASE) ** (-(np.arange(half, dtype=np.float32) * np.float32(2.0 / HD)))
    angle = (np.arange(SEQ, dtype=np.float32)[:, None] * freq[None, :]).astype(np.float64)
    cos, sin = np.cos(angle), np.sin(angle)
    return (
        np.concatenate([cos, cos], axis=1).astype(np.float32),
        np.concatenate([-sin, sin], axis=1).astype(np.float32),
    )


def eye(n):
    return lax.broadcasted_iota(jnp.int32, (n, n), 0) == lax.broadcasted_iota(jnp.int32, (n, n), 1)


def to_column(row, diag):
    return jnp.sum(jnp.where(diag, row, 0.0), axis=1, keepdims=True)


def to_row(column, diag):
    return jnp.sum(jnp.where(diag, column, 0.0), axis=0, keepdims=True)


def two_halves(row):
    lead = row.astype(BF)
    rest = (row - lead.astype(F32)).astype(BF)
    at = lax.broadcasted_iota(jnp.int32, (16, HD), 0)
    zero = jnp.zeros((), F32)
    both = jnp.where(at == 0, lead.astype(F32), jnp.where(at == 1, rest.astype(F32), zero))
    return both.astype(BF)


def from_halves(tile):
    both = tile.astype(F32)
    return both[0:1, :] + both[1:2, :]


def turn(vec, cos, sin):
    return vec * cos + pltpu.roll(vec, HD // 2, 1) * sin


def turn_back(vec, cos, sin):
    return vec * cos - pltpu.roll(vec, HD // 2, 1) * sin


def total_of(got_ref):
    total = got_ref[0].astype(F32)
    for at in range(1, got_ref.shape[0]):
        total += got_ref[at].astype(F32)
    return total


def project_kernel(
    step, hid_hbm, gain_hbm, wk_hbm, wv_hbm, q_hbm, seg_hbm, cos_hbm, sin_hbm,
    out_ref, send_ref, keep_ref, q_rot_ref, bias_ref, angle_ref,
    hid_ref, gain_ref, wk_ref, wv_ref, q_ref, seg_ref, cos_ref, sin_ref, scaled_ref, turned_ref, sem
):
    quarters = SEQ // Q
    feats = hid_ref.shape[1]
    gain_copy = pltpu.make_async_copy(gain_hbm, gain_ref, sem.at[0])
    hid_copies = []
    for at in range(quarters):
        rows = pl.ds(at * Q, Q)
        hid_copies.append(pltpu.make_async_copy(hid_hbm.at[rows, :], hid_ref.at[rows, :], sem.at[1 + at]))
    weight_copies = [
        pltpu.make_async_copy(wk_hbm, wk_ref, sem.at[5]),
        pltpu.make_async_copy(wv_hbm, wv_ref, sem.at[6]),
    ]
    late_copies = [
        pltpu.make_async_copy(src, dst, sem.at[7 + at])
        for at, (src, dst) in enumerate(
            ((q_hbm, q_ref), (seg_hbm, seg_ref), (cos_hbm, cos_ref), (sin_hbm, sin_ref))
        )
    ]
    for copy in [gain_copy] + hid_copies + weight_copies + late_copies:
        copy.start()
    ones = jnp.ones((16, HD), BF)
    gain_copy.wait()
    for quarter in range(quarters):
        hid_copies[quarter].wait()
        rows = slice(quarter * Q, (quarter + 1) * Q)
        hid = hid_ref[rows, :].astype(F32)
        scaled_ref[rows, :] = (hid * gain_ref[...]).astype(BF)
        turned_ref[:, rows] = hid.T.astype(BF)
        square = hid * hid
        square = sum(square[:, c * HD : (c + 1) * HD] for c in range(feats // HD))
        lead = square.astype(BF)
        rest = (square - lead.astype(F32)).astype(BF)
        sums = lax.dot_general(ones, lead, NT, preferred_element_type=F32)
        sums += lax.dot_general(ones, rest, NT, preferred_element_type=F32)
        tile = two_halves(sums[0:1, :])
        for head in range(KVH):
            out_ref[head * quarters + quarter, 2 * Q : CH, :] = tile
    for which, weight_ref in enumerate((wk_ref, wv_ref)):
        weight_copies[which].wait()
        part = jnp.dot(scaled_ref[...], weight_ref[...], preferred_element_type=F32).astype(BF)
        for quarter in range(quarters):
            for head in range(KVH):
                out_ref[head * quarters + quarter, which * Q : (which + 1) * Q, :] = part[
                    quarter * Q : (quarter + 1) * Q, head * HD : (head + 1) * HD
                ]
    core = lax.axis_index("core")
    for which in range(2):
        parity = lax.axis_index("zl") if which == 0 else 1 - lax.axis_index("zl")
        for at in range(keep_ref.shape[1] // step):
            mine = pl.multiple_of((4 * at + 2 * parity + core) * step, step)
            other = pl.multiple_of((4 * at + 2 * parity + 1 - core) * step, step)
            rows = slice(at * step, (at + 1) * step)
            keep_ref[which, rows, :] = turned_ref[pl.ds(mine, step), :]
            send_ref[which, rows, :] = turned_ref[pl.ds(other, step), :]
    for copy in late_copies:
        copy.wait()
    own = pl.ds(pl.multiple_of(lax.axis_index("y") * Q, Q), Q)
    angle_ref[0] = cos_ref[own, :]
    angle_ref[1] = sin_ref[own, :]
    diag = eye(Q)
    below = lax.broadcasted_iota(jnp.int32, (Q, Q), 0) <= lax.broadcasted_iota(
        jnp.int32, (Q, Q), 1
    )
    seg_rows = [seg_ref[0:1, b * Q : (b + 1) * Q].astype(F32) for b in range(quarters)]
    seg_columns = [to_column(row, diag) for row in seg_rows]
    for b, (low, first) in enumerate(spans()[0]):
        rows = slice(b * Q, (b + 1) * Q)
        cos, sin = cos_ref[rows, :], sin_ref[rows, :]
        for h in range(2):
            turned = turn(q_ref[rows, h * HD : (h + 1) * HD].astype(F32), cos, sin)
            q_rot_ref[b, h * Q : (h + 1) * Q, :] = turned.astype(BF)
        for a in range(low, b + 1):
            same = seg_columns[a] == seg_rows[b]
            allowed = same & below if a == b else same
            at = first + (a - low) * Q
            bias_ref[at : at + Q, :] = jnp.where(allowed, 0.0, -1e30)


def combine_kernel(got_ref, angle_ref, out_ref):
    total = total_of(got_ref)
    square = total[2 * Q : 2 * Q + 1, :] + total[2 * Q + 1 : 2 * Q + 2, :]
    inv_row = lax.rsqrt(square / D + 1e-05)
    inv = to_column(inv_row, eye(Q))
    keys = (total[:Q, :] * inv).astype(BF).astype(F32)
    keys = turn(keys, angle_ref[0], angle_ref[1]).astype(BF)
    values = (total[Q : 2 * Q, :] * inv).astype(BF)
    tile = two_halves(inv_row)
    for at in range(out_ref.shape[0]):
        out_ref[at, 0:Q, :] = keys
        out_ref[at, Q : 2 * Q, :] = values
        out_ref[at, 2 * Q : CH, :] = tile


def spans():
    found, first = [], 0
    for b in range(SEQ // Q):
        low = max(0, b - 2)
        found.append((low, first))
        first += (b + 1 - low) * Q
    return found, first


def attention_kernel(kv_ref, q_rot_ref, cot_ref, bias_ref, gkv_ref, probs_ref, ds_ref):
    blocks = SEQ // Q
    cots = []
    for b, (low, first) in enumerate(spans()[0]):
        rows = slice(b * Q, (b + 1) * Q)
        keys = jnp.concatenate([kv_ref[a, 0:Q, :] for a in range(low, b + 1)], axis=0)
        values = jnp.concatenate([kv_ref[a, Q : 2 * Q, :] for a in range(low, b + 1)], axis=0)
        q_rot = q_rot_ref[b]
        cot = jnp.concatenate([cot_ref[rows, 0:HD], cot_ref[rows, HD:]], axis=0)
        cots.append(cot)
        kept = slice(first, first + (b + 1 - low) * Q)
        bias = jnp.concatenate([bias_ref[kept, :]] * 2, axis=1)
        scores = lax.dot_general(keys, q_rot, NT, preferred_element_type=F32) + bias
        top = jnp.max(scores, axis=0, keepdims=True)
        expo = jnp.exp((scores - top) * SCALE)
        probs = (expo * (1.0 / jnp.sum(expo, axis=0, keepdims=True))).astype(BF)
        d_probs = lax.dot_general(values, cot, NT, preferred_element_type=F32)
        prob_float = probs.astype(F32)
        delta = jnp.sum(prob_float * d_probs, axis=0, keepdims=True)
        probs_ref[kept, :] = probs
        ds_ref[kept, :] = (prob_float * (d_probs - delta)).astype(BF)
    for a in range(blocks):
        wide, deep, queries, cotangents = [], [], [], []
        for b, (low, first) in enumerate(spans()[0]):
            if low <= a <= b:
                at = first + (a - low) * Q
                wide.append(probs_ref[at : at + Q, :])
                deep.append(ds_ref[at : at + Q, :])
                queries.append(q_rot_ref[b])
                cotangents.append(cots[b])
        wide, deep = jnp.concatenate(wide, axis=1), jnp.concatenate(deep, axis=1)
        queries, cotangents = jnp.concatenate(queries, axis=0), jnp.concatenate(cotangents, axis=0)
        d_values = jnp.dot(wide, cotangents, preferred_element_type=F32)
        d_keys = jnp.dot(deep, queries, preferred_element_type=F32)
        gkv_ref[a, 0:Q, :] = (d_keys * SCALE).astype(BF)
        gkv_ref[a, Q : 2 * Q, :] = d_values.astype(BF)


def outputs_kernel(kv_ref, probs_ref, ds_ref, cos_ref, sin_ref, out_ref, gq_ref):
    for b, (low, first) in enumerate(spans()[0]):
        rows = slice(b * Q, (b + 1) * Q)
        keys = jnp.concatenate([kv_ref[a, 0:Q, :] for a in range(low, b + 1)], axis=0)
        values = jnp.concatenate([kv_ref[a, Q : 2 * Q, :] for a in range(low, b + 1)], axis=0)
        cos, sin = cos_ref[rows, :], sin_ref[rows, :]
        kept = slice(first, first + (b + 1 - low) * Q)
        attn = lax.dot_general(probs_ref[kept, :], values, TN, preferred_element_type=F32)
        d_q = lax.dot_general(ds_ref[kept, :], keys, TN, preferred_element_type=F32)
        for h in range(2):
            cols = slice(h * HD, (h + 1) * HD)
            out_ref[rows, cols] = attn[h * Q : (h + 1) * Q].astype(BF)
            d_query = d_q[h * Q : (h + 1) * Q] * SCALE
            gq_ref[rows, cols] = turn_back(d_query, cos, sin).astype(BF)


def grad_sum_kernel(got_ref, kv_ref, angle_ref, out_ref):
    total = total_of(got_ref)
    own = kv_ref[0, 0 : 2 * Q, :].astype(F32)
    both = total * own
    corr = to_row(jnp.sum(both[:Q] + both[Q:], axis=1, keepdims=True), eye(Q))
    d_keys = turn_back(total[:Q, :], angle_ref[0], angle_ref[1])
    inv = to_column(from_halves(kv_ref[0, 2 * Q : CH, :]), eye(Q))
    d_keys = (d_keys * inv).astype(BF)
    d_values = (total[Q:, :] * inv).astype(BF)
    tile = two_halves(corr)
    for at in range(out_ref.shape[0]):
        out_ref[at, 0:Q, :] = d_keys
        out_ref[at, Q : 2 * Q, :] = d_values
        out_ref[at, 2 * Q : CH, :] = tile


def weight_kernel(got_ref, turned_ref, out_ref):
    blocks = SEQ // Q
    width = KVH * HD
    for which in range(2):
        for pair in range(KVH // 2):
            columns = []
            for head in (2 * pair, 2 * pair + 1):
                part = [
                    got_ref[head * blocks + b, which * Q : (which + 1) * Q, :] for b in range(blocks)
                ]
                columns.append(jnp.concatenate(part, axis=0))
            grads = jnp.concatenate(columns, axis=1)
            at = which * width + 2 * pair * HD
            for parity in range(2):
                product = jnp.dot(turned_ref[parity], grads, preferred_element_type=F32)
                out_ref[parity, :, at : at + 2 * HD] = product.astype(BF)


def hidden_kernel(got_ref, kv_ref, hid_ref, gain_ref, wk_ref, wv_ref, out_ref):
    blocks = SEQ // Q
    diag = eye(Q)
    wk, wv = wk_ref[...], wv_ref[...]
    for b in range(blocks):
        rows = slice(b * Q, (b + 1) * Q)
        mine = [got_ref[head * blocks + b] for head in range(KVH)]
        d_keys = jnp.concatenate([m[0:Q] for m in mine], axis=1)
        d_values = jnp.concatenate([m[Q : 2 * Q] for m in mine], axis=1)
        inv = to_column(from_halves(kv_ref[b, 2 * Q : CH, :]), diag)
        corr = sum(from_halves(m[2 * Q : CH]) for m in mine)
        corr = to_column(corr, diag) / D
        d_normed = lax.dot_general(d_keys, wk, NT, preferred_element_type=F32)
        d_normed += lax.dot_general(d_values, wv, NT, preferred_element_type=F32)
        hid = hid_ref[rows, :].astype(F32)
        out_ref[rows, :] = (d_normed * gain_ref[...] - hid * (inv * inv * corr)).astype(BF)


def pair_kernel(keep_ref, got_ref, out_ref):
    out_ref[...] = (keep_ref[1].astype(F32) + got_ref[1].astype(F32)).astype(BF)


def four_kernel(keep_ref, got_ref, next_ref, out_ref):
    total = keep_ref[0].astype(F32) + got_ref[0].astype(F32) + next_ref[...].astype(F32)
    out_ref[...] = total.astype(BF)


def own_rows_kernel(gain_ref, wk_ref, wv_ref, out_ref):
    step, width = out_ref.shape[0], KVH * HD
    place = (lax.axis_index("zh") * 2 + lax.axis_index("zl")) * 2 + lax.axis_index("core")
    first = pl.multiple_of(place * step, step)
    lanes = lax.broadcasted_iota(jnp.int32, (step, gain_ref.shape[1]), 1)
    rows = lax.broadcasted_iota(jnp.int32, (step, gain_ref.shape[1]), 0)
    gain = jnp.sum(jnp.where(lanes == rows + first, gain_ref[...], 0.0), axis=1, keepdims=True)
    out_ref[:, 0:width] = wk_ref[pl.ds(first, step), :].astype(F32)
    out_ref[:, width : 2 * width] = wv_ref[pl.ds(first, step), :].astype(F32)
    out_ref[:, 2 * width :] = jnp.broadcast_to(gain, (step, HD))


def finish_kernel(got_ref, rows_ref, gk_ref, gv_ref, gg_ref):
    step, width = gk_ref.shape
    total = total_of(got_ref)
    gain = rows_ref[:, 2 * width : 2 * width + 1]
    gk_ref[...] = total[:, :width] * gain
    gv_ref[...] = total[:, width:] * gain
    along = rows_ref[:, 0 : 2 * width] * total
    gg_ref[...] = to_row(jnp.sum(along, axis=1, keepdims=True), eye(step))


def neighbours(nz):
    pairs = []
    for z in range(nz):
        for core in range(2):
            other = (z ^ 1) if core == 0 else ((z + nz - 1) % nz if z % 2 == 0 else (z + 1) % nz)
            pairs.append((2 * z + core, 2 * other + core))
    return pairs


def in_hbm(array):
    return pltpu.with_memory_space_constraint(array, pltpu.HBM)


VMEM = pl.BlockSpec(memory_space=pltpu.VMEM)
HBM = pl.BlockSpec(memory_space=pltpu.HBM)


def call(kernel, name, out_shape, in_specs, out_specs=None, scratch=(), cost=None, grant=16):
    many = isinstance(out_shape, (list, tuple))
    if out_specs is None:
        out_specs = [VMEM] * len(out_shape) if many else VMEM
    flops, size = cost
    return pl.pallas_call(
        kernel,
        out_shape=out_shape,
        in_specs=in_specs,
        out_specs=out_specs,
        scratch_shapes=list(scratch),
        compiler_params=pltpu.CompilerParams(vmem_limit_bytes=grant * 1024 * 1024),
        cost_estimate=pl.CostEstimate(flops=int(flops), bytes_accessed=int(size), transcendentals=0),
        name=name,
    )


def body(nz, hidden_in, norm_gain, key_weight, value_weight, queries, segments, cotangent):
    shape = jax.ShapeDtypeStruct
    width = KVH * HD
    feats = hidden_in.shape[1]
    step = feats // (2 * nz)
    quarter = feats // 4
    blocks = SEQ // Q
    kept = spans()[1]
    dma = pltpu.SemaphoreType.DMA
    cos, sin = (jnp.asarray(t) for t in rope_tables())
    gain = norm_gain.reshape(1, feats)

    parts, turned_send, turned_keep, q_rot, bias, angle = call(
        functools.partial(project_kernel, step),
        "project",
        [
            shape((KVH * blocks, CH, HD), BF),
            shape((2, quarter, SEQ), BF),
            shape((2, quarter, SEQ), BF),
            shape((blocks, 2 * Q, HD), BF),
            shape((kept, Q), F32),
            shape((2, Q, HD), F32),
        ],
        [HBM] * 8,
        scratch=[
            pltpu.VMEM((SEQ, feats), BF),
            pltpu.VMEM((1, feats), F32),
            pltpu.VMEM((feats, width), BF),
            pltpu.VMEM((feats, width), BF),
            pltpu.VMEM(queries.shape, BF),
            pltpu.VMEM(segments.shape, jnp.int32),
            pltpu.VMEM((SEQ, HD), F32),
            pltpu.VMEM((SEQ, HD), F32),
            pltpu.VMEM((SEQ, feats), BF),
            pltpu.VMEM((feats, SEQ), BF),
            dma((11,)),
        ],
        cost=(4 * SEQ * feats * width, 4e6),
    )(*(in_hbm(a) for a in (hidden_in, gain, key_weight, value_weight, queries, segments, cos, sin)))
    parts = lax.all_to_all(parts, ("x", "y"), 0, 0, tiled=True)
    own = call(
        combine_kernel,
        "combine",
        shape((blocks, CH, HD), BF),
        [VMEM] * 2,
        cost=(16 * CH * HD, 1.5e6),
    )(parts, angle)
    kv = lax.all_to_all(own, "y", 0, 0, tiled=True)
    grad_parts, probs, d_scores = call(
        attention_kernel,
        "attention",
        [shape((blocks, 2 * Q, HD), BF), shape((kept, 2 * Q), BF), shape((kept, 2 * Q), BF)],
        [VMEM] * 4,
        cost=(8 * kept * 2 * Q * HD, 2e6),
    )(kv, q_rot, cotangent, bias)
    grad_parts = lax.all_to_all(grad_parts, "y", 0, 0, tiled=True)
    grad_own = call(
        grad_sum_kernel,
        "grad_sum",
        shape((KVH * blocks, CH, HD), BF),
        [VMEM] * 3,
        cost=(16 * CH * HD, 1.5e6),
    )(grad_parts, own, angle)
    grads = lax.all_to_all(grad_own, ("x", "y"), 0, 0, tiled=True)

    def product(turned, name):
        return call(
            weight_kernel,
            name,
            shape((2, quarter, 2 * width), BF),
            [VMEM] * 2,
            cost=(4 * SEQ * feats // 2 * width, 2e6),
        )(grads, turned)

    swap = [(0, 1), (1, 0)]
    send = product(turned_send, "weight_send")
    send, turned_keep = lax.optimization_barrier((send, turned_keep))
    got = lax.ppermute(send, "core", swap)
    keep = product(turned_keep, "weight_keep")
    pair = call(
        pair_kernel,
        "pair",
        shape((quarter, 2 * width), BF),
        [VMEM] * 2,
        cost=(quarter * 2 * width, 1e6),
    )(keep, got)
    pair, probs, grads, gain_late = lax.optimization_barrier((pair, probs, grads, gain))
    got_pair = lax.ppermute(pair, ("zh", "zl", "core"), neighbours(nz))
    own_rows = call(
        own_rows_kernel,
        "own_rows",
        shape((step, 2 * width + HD), F32),
        [VMEM] * 3,
        cost=(SEQ * feats, 1e6),
    )(gain_late, key_weight, value_weight)
    grad_hidden = call(
        hidden_kernel,
        "hidden",
        shape(hidden_in.shape, BF),
        [VMEM] * 6,
        cost=(4 * SEQ * feats * width, 4e6),
    )(grads, kv, hidden_in, gain, key_weight, value_weight)
    attn_out, grad_queries = call(
        outputs_kernel,
        "outputs",
        [shape(queries.shape, BF), shape(queries.shape, BF)],
        [VMEM] * 5,
        cost=(4 * kept * 2 * Q * HD, 2e6),
    )(kv, probs, d_scores, cos, sin)
    got_pair, grad_hidden, attn_out, grad_queries, own_rows = lax.optimization_barrier(
        (got_pair, grad_hidden, attn_out, grad_queries, own_rows)
    )
    four = call(
        four_kernel,
        "four",
        shape((quarter, 2 * width), BF),
        [VMEM] * 3,
        cost=(quarter * 2 * width, 1e6),
    )(keep, got, got_pair)
    rows = lax.all_to_all(four.reshape(nz // 2, step, 2 * width), "zh", 0, 0, tiled=True)
    grad_key, grad_value, grad_gain = call(
        finish_kernel,
        "finish",
        [shape((step, width), F32), shape((step, width), F32), shape((1, step), F32)],
        [VMEM] * 2,
        cost=(quarter * 2 * width, 1e6),
    )(rows, own_rows)
    return (attn_out, grad_hidden, grad_queries, grad_key, grad_value, grad_gain.reshape(step))


def solution(mesh):
    nz = mesh.devices.shape[0] // 2
    split = Mesh(mesh.devices.reshape(nz // 2, 2, 2, 4, 4), ("zh", "zl", "core", "x", "y"))
    dp, tensor = ("zh", "zl", "core"), ("x", "y")
    return jax.shard_map(
        functools.partial(body, nz),
        mesh=split,
        in_specs=(
            P(dp, tensor),
            P(tensor),
            P(tensor, None),
            P(tensor, None),
            P(dp, tensor),
            P(dp, None),
            P(dp, tensor),
        ),
        out_specs=(
            P(dp, tensor),
            P(dp, tensor),
            P(dp, tensor),
            P(tensor + dp, None),
            P(tensor + dp, None),
            P(tensor + dp),
        ),
        check_vma=False,
    )
```

time: 121 us -> 116 us (0.959)
  the two profiles are of different devices: /device:TPU:6 before, /device:TPU:1 now
where the time goes in v3:
time: 116 us; the launch traced here: 115 us
  blocking collectives  82.8 us (71%)
  starting transfers between devices  20.5 us (18%)
  Pallas kernels  10.2 us (9%)
    all_to_all x1, blocking collectives, body(): lax.all_to_all(four.reshape(nz // 2, step, 2 * width), 'zh', 0, 0, tiled=...  28.6 us
    all_to_all x1, blocking collectives, body(): parts = lax.all_to_all(parts, ('x', 'y'), 0, 0, tiled=True)  22.8 us
    all_to_all x1, blocking collectives, body(): grads = lax.all_to_all(grad_own, ('x', 'y'), 0, 0, tiled=True)  15.3 us
    ppermute x1, starting transfers between devices, body(): got_pair = lax.ppermute(pair, ('zh', 'zl', 'core'), neighbours(nz))  12 us
    ppermute x1, starting transfers between devices, body(): got = lax.ppermute(send, 'core', swap)  8.52 us
    all_to_all x1, blocking collectives, body(): kv = lax.all_to_all(own, 'y', 0, 0, tiled=True)  8.16 us
    all_to_all x1, blocking collectives, body(): grad_parts = lax.all_to_all(grad_parts, 'y', 0, 0, tiled=True)  7.92 us
    pallas_call x1, Pallas kernels, body(): call(functools.partial(project_kernel, step), 'project', [shape((KVH * bl...  3.01 us
  transfers between devices with their start and end apart: 2, of which 1 were waited for; matrix products, arithmetic and copies ran while one was open for 0% of the time, Pallas kernels for 4%

profile of v3, /device:TPU:1, one launch (start us, length us, event | category | flops | bytes accessed | tf_op | source)
XLA Modules:
  0.0 115.4 jit_solution(1854004988398561377)
XLA Ops:
  0.6 3.0 %project.1 = (bf16[16,272,128]{2,1,0:T(8,128)(2,1)S(1)}, bf16[2,128,512]{2,1,0:T(8,128)(2,1)S(1)}, bf16[2,128,512]{2,1,0:T(8,128)(2,1)S(1)}, bf16[4,256,128]{2,1...) custom-call(bf16[512,512]{1,0:T(8,128)(2,1)} %hid_ref.1, f32[1,512]{1,0:T(1,128)} %bitcast.4, ...), custom_call_target="tpu_custom_call" | custom-call | flops 536870912 | bytes 4000000 | tf_op jit(solution)/shard_map/project/pallas_call | solution.py:366
  3.6 22.8 %all_to_all.25.got_ref = bf16[16,272,128]{2,1,0:T(8,128)(2,1)S(1)} all-to-all(bf16[16,272,128]{2,1,0:T(8,128)(2,1)S(1)} %get-tuple-element.31), channel_id=1, replica_groups=mesh['zh'=8,'zl'=2,'core'=2,'x'=4,'y'=4] {'x','y'}, dimensions={0} | all-to-all | bytes 2228224 | tf_op jit(solution)/shard_map/all_to_all | solution.py:393
  26.4 0.2 combine.1.kv_ref
  26.7 8.2 %all_to_all.26.kv_ref = bf16[4,272,128]{2,1,0:T(8,128)(2,1)S(1)} all-to-all(bf16[4,272,128]{2,1,0:T(8,128)(2,1)S(1)} %combine.1.kv_ref), channel_id=1, replica_groups=mesh['zh'=8,'zl'=2,'core'=2,'x'=4,'y'=4] {'y'}, dimensions={0} | all-to-all | bytes 557056 | tf_op jit(solution)/shard_map/all_to_all | solution.py:401
  34.8 0.0 copy-done.5
  34.8 1.3 %attention.1 = (bf16[4,256,128]{2,1,0:T(8,128)(2,1)S(1)}, bf16[1152,256]{1,0:T(8,128)(2,1)S(1)}, bf16[1152,256]{1,0:T(8,128)(2,1)S(1)}) custom-call(bf16[4,272,128]{2,1,0:T(8,128)(2,1)S(1)} %all_to_all.26.kv_ref, bf16[4,256,128]{2,1,0:T(8,128)(2,1)S(1)} %get-tuple-element.33.q_rot_ref, bf16[512,256]{1,0:T(8,128)(2,1)S(1)} %copy-done.5, ...), custom_call_target="tpu_custom_call" | custom-call | flops 301989888 | bytes 2000000 | tf_op jit(solution)/shard_map/attention/pallas_call | solution.py:402
  36.1 7.9 %all_to_all.27.got_ref = bf16[4,256,128]{2,1,0:T(8,128)(2,1)S(1)} all-to-all(bf16[4,256,128]{2,1,0:T(8,128)(2,1)S(1)} %get-tuple-element.35), channel_id=1, replica_groups=mesh['zh'=8,'zl'=2,'core'=2,'x'=4,'y'=4] {'y'}, dimensions={0} | all-to-all | bytes 524288 | tf_op jit(solution)/shard_map/all_to_all | solution.py:409
  44.1 0.2 grad_sum.1
  44.3 15.3 %all_to_all.28.got_ref = bf16[16,272,128]{2,1,0:T(8,128)(2,1)S(1)} all-to-all(bf16[16,272,128]{2,1,0:T(8,128)(2,1)S(1)} %grad_sum.1), channel_id=1, replica_groups=mesh['zh'=8,'zl'=2,'core'=2,'x'=4,'y'=4] {'x','y'}, dimensions={0} | all-to-all | bytes 2228224 | tf_op jit(solution)/shard_map/all_to_all | solution.py:417
  59.6 0.4 weight_send.1
  60.1 8.5 %collective-permute-start = (bf16[2,128,1024]{2,1,0:T(8,128)(2,1)S(1)}, bf16[2,128,1024]{2,1,0:T(8,128)(2,1)S(1)}, u32[]{:S(2)}, u32[]{:S(2)}) collective-permute-start(bf16[2,128,1024]{2,1,0:T(8,128)(2,1)S(1)} %weight_send.1), channel_id=1, source_target_pairs={{0,16},{16,0},{1,17},{17,1},{2,18},{18,2},{3,19},{19,3},{4,20},{20... | collective-permute-start | bytes 1572872 | tf_op jit(solution)/shard_map/ppermute | solution.py:431
  68.6 0.0 copy-start.6
  68.6 0.4 weight_keep.1.keep_ref
  69.0 0.0 copy-start
  69.1 0.0 copy-start.1
  69.1 0.0 copy-start.3
  69.1 0.0 copy-start.4
  69.1 1.0 collective-permute-done.got_ref
  70.1 0.1 pair.1
  70.2 12.0 %collective-permute-start.1 = (bf16[128,1024]{1,0:T(8,128)(2,1)S(1)}, bf16[128,1024]{1,0:T(8,128)(2,1)S(1)}, u32[]{:S(2)}, u32[]{:S(2)}) collective-permute-start(bf16[128,1024]{1,0:T(8,128)(2,1)S(1)} %pair.1), channel_id=1, source_target_pairs={{0,32},{16,496},{32,0},{48,80},{64,96},{80,48},{96,64},{112,144},{... | collective-permute-start | bytes 786440 | tf_op jit(solution)/shard_map/ppermute | solution.py:441
  82.2 0.0 copy-done.6
  82.2 0.0 copy-done
  82.2 0.0 copy-done.1
  82.2 0.1 own_rows.1.rows_ref
  82.3 0.0 copy-done.3
  82.3 0.0 copy-done.4
  82.3 1.3 %outputs.1 = (bf16[512,256]{1,0:T(8,128)(2,1)}, bf16[512,256]{1,0:T(8,128)(2,1)}) custom-call(bf16[4,272,128]{2,1,0:T(8,128)(2,1)S(1)} %all_to_all.26.kv_ref, bf16[1152,256]{1,0:T(8,128)(2,1)S(1)} %get-tuple-element.43.probs_ref, bf16[1152,256]{1,0:T(8,128)(2,1)S(1)} %get-tuple-element.44.ds_ref, f32[512,128]{1,0:T(8,128)S(1)} %copy-done.4, ...), custom_call_target="tpu_custom_call" | custom-call | flops 150994944 | bytes 2000000 | tf_op jit(solution)/shard_map/outputs/pallas_call | solution.py:456
  83.6 2.3 %hidden.1 = bf16[512,512]{1,0:T(8,128)(2,1)} custom-call(bf16[16,272,128]{2,1,0:T(8,128)(2,1)S(1)} %all_to_all.28.got_ref, bf16[4,272,128]{2,1,0:T(8,128)(2,1)S(1)} %all_to_all.26.kv_ref, bf16[512,512]{1,0:T(8,128)(2,1)S(1)} %copy-done.2, f32[1,512]{1,0:T(1,128)S(1)} %bitcast.6, bf16[512,512]{1,0:T(8,128)(2,1)S(1)} %copy-done, bf16[512,512]{1,0:T(8,128)(2,1)S(1)} %copy-done.1), custom_call_target="tpu_custom_call" | custom-call | flops 536870912 | bytes 4000000 | tf_op jit(solution)/shard_map/hidden/pallas_call | solution.py:449
  85.9 0.0 collective-permute-done.1.next_ref
  85.9 0.1 four.1
  86.0 28.6 %all_to_all.29.got_ref = bf16[8,16,1024]{2,1,0:T(8,128)(2,1)S(1)} all-to-all(bf16[8,16,1024]{2,1,0:T(8,128)(2,1)S(1)} %bitcast.3), channel_id=1, replica_groups=mesh['zh'=8,'zl'=2,'core'=2,'x'=4,'y'=4] {'zh'}, dimensions={0} | all-to-all | bytes 524288 | tf_op jit(solution)/shard_map/all_to_all | solution.py:473
  114.7 0.7 finish.1
  (3 shorter events, 0.0 us)
Async XLA Ops:
  26.4 8.4 %copy-start.5 = (bf16[512,256]{1,0:T(8,128)(2,1)S(1)}, bf16[512,256]{1,0:T(8,128)(2,1)}, u32[]{:S(2)}) copy-start(bf16[512,256]{1,0:T(8,128)(2,1)} %cot_ref.1) | copy-start | bytes 786436
  60.1 10.0 %collective-permute-start = (bf16[2,128,1024]{2,1,0:T(8,128)(2,1)S(1)}, bf16[2,128,1024]{2,1,0:T(8,128)(2,1)S(1)}, u32[]{:S(2)}, u32[]{:S(2)}) collective-permute-start(bf16[2,128,1024]{2,1,0:T(8,128)(2,1)S(1)} %weight_send.1), channel_id=1, source_target_pairs={{0,16},{16,0},{1,17},{17,1},{2,18},{18,2},{3,19},{19,3},{4,20},{20... | collective-permute-start | bytes 1572872 | tf_op jit(solution)/shard_map/ppermute | solution.py:431
  68.6 13.6 %copy-start.6 = (f32[512]{0:T(512)S(1)}, f32[512]{0:T(512)}, u32[]{:S(2)}) copy-start(f32[512]{0:T(512)} %param.10) | copy-start | bytes 6148
  69.0 13.2 %copy-start = (bf16[512,512]{1,0:T(8,128)(2,1)S(1)}, bf16[512,512]{1,0:T(8,128)(2,1)}, u32[]{:S(2)}) copy-start(bf16[512,512]{1,0:T(8,128)(2,1)} %wk_ref.3) | copy-start | bytes 1572868
  69.1 13.2 %copy-start.1 = (bf16[512,512]{1,0:T(8,128)(2,1)S(1)}, bf16[512,512]{1,0:T(8,128)(2,1)}, u32[]{:S(2)}) copy-start(bf16[512,512]{1,0:T(8,128)(2,1)} %wv_ref.3) | copy-start | bytes 1572868
  69.1 13.3 %copy-start.3 = (f32[512,128]{1,0:T(8,128)S(1)}, f32[512,128]{1,0:T(8,128)}, u32[]{:S(2)}) copy-start(f32[512,128]{1,0:T(8,128)} %constant.5.clone.sin_hbm.sin_ref) | copy-start | bytes 786436
  69.1 13.3 %copy-start.4 = (f32[512,128]{1,0:T(8,128)S(1)}, f32[512,128]{1,0:T(8,128)}, u32[]{:S(2)}) copy-start(f32[512,128]{1,0:T(8,128)} %constant.4.clone.cos_hbm.cos_ref) | copy-start | bytes 786436
  70.2 15.8 %collective-permute-start.1 = (bf16[128,1024]{1,0:T(8,128)(2,1)S(1)}, bf16[128,1024]{1,0:T(8,128)(2,1)S(1)}, u32[]{:S(2)}, u32[]{:S(2)}) collective-permute-start(bf16[128,1024]{1,0:T(8,128)(2,1)S(1)} %pair.1), channel_id=1, source_target_pairs={{0,32},{16,496},{32,0},{48,80},{64,96},{80,48},{96,64},{112,144},{... | collective-permute-start | bytes 786440 | tf_op jit(solution)/shard_map/ppermute | solution.py:441
  82.3 1.3 %copy-start.2 = (bf16[512,512]{1,0:T(8,128)(2,1)S(1)}, bf16[512,512]{1,0:T(8,128)(2,1)}, u32[]{:S(2)}) copy-start(bf16[512,512]{1,0:T(8,128)(2,1)} %hid_ref.1) | copy-start | bytes 1572868
